TPU v7x, 32 devices: a whole 2x2x4 slice. The times are simulated.
32 devices in a mesh: node: 8 (over y, x, core), local: 4 (over z).
Axes of the slice: x: 2, y: 2, z: 4, core: 2. Of those that a mesh axis runs over, the one named last changes fastest.
Arguments:
- tokens: bfloat16 [2048, 4096], P('local'), may hold values from -6 to 6
- cotangent: bfloat16 [2048, 4096], P('local'), may hold values from -6 to 6
- gate_weight: bfloat16 [4096, 12288], P('local', 'node'), may hold values from -0.125 to 0.125
- up_weight: bfloat16 [4096, 12288], P('local', 'node'), may hold values from -0.125 to 0.125
- down_weight: bfloat16 [12288, 4096], P('node', 'local'), may hold values from -0.078125 to 0.078125
Outputs:
- block_out: bfloat16 [2048, 4096], P('local', 'node')
- input_grad: bfloat16 [2048, 4096], P('local', 'node')
- gate_grad: float32 [4096, 12288], P('local', 'node')
- up_grad: float32 [4096, 12288], P('local', 'node')
- down_grad: float32 [12288, 4096], P('node', 'local')
All inputs are finite; a program needn't handle non-finite values.
Results may differ from a plain program's by a relative error of at most 0.013.
Values may be sent and summed in bfloat16 or wider, within the bound.
No kernel may reach another device: no remote copies, remote signals or barrier semaphores. Data moves between devices by JAX's collectives and lax.ppermute only.
A program may use at most 384 MiB of HBM per device.

v0:
```python
import math

import jax
import jax.numpy as jnp
from jax import lax
from jax.sharding import PartitionSpec as P


def forward_gates(gate_part, up_part):
    sigma = jax.nn.sigmoid(gate_part)
    active = gate_part * sigma
    hidden = (active * up_part).astype(jnp.bfloat16)
    return (sigma, active, hidden)


def backward_gates(hidden_back, gate_part, up_part, sigma, active):
    gate_back = (hidden_back * up_part * sigma * (1.0 + gate_part * (1.0 - sigma))).astype(
        jnp.bfloat16
    )
    up_back = (hidden_back * active).astype(jnp.bfloat16)
    return (gate_back, up_back)


def contract_last(left, right):
    return lax.dot_general(
        left, right, (((1,), (1,)), ((), ())), preferred_element_type=jnp.float32
    )


def contract_first(left, right):
    return lax.dot_general(
        left, right, (((0,), (0,)), ((), ())), preferred_element_type=jnp.float32
    )


def per_device(tokens, cotangent, gate_weight, up_weight, down_weight):
    tok_rows = tokens.shape[0]
    unit_count = gate_weight.shape[1]
    groups = lax.axis_size("local")
    grad_scale = 1.0 / math.sqrt(tok_rows * groups)
    full_gate, full_up, full_down = (
        lax.all_gather(gate_weight, "local", axis=0, tiled=True),
        lax.all_gather(up_weight, "local", axis=0, tiled=True),
        lax.all_gather(down_weight, "local", axis=1, tiled=True),
    )
    gate_part = jnp.dot(tokens, full_gate, preferred_element_type=jnp.float32)
    up_part = jnp.dot(tokens, full_up, preferred_element_type=jnp.float32)
    sigma, active, hidden = forward_gates(gate_part, up_part)
    out_terms = jnp.dot(hidden, full_down, preferred_element_type=jnp.float32)
    block_out = lax.psum_scatter(
        out_terms.astype(jnp.bfloat16), "node", scatter_dimension=1, tiled=True
    )
    hidden_back = contract_last(cotangent, full_down)
    gate_back, up_back = backward_gates(hidden_back, gate_part, up_part, sigma, active)
    input_terms = contract_last(gate_back, full_gate) + contract_last(up_back, full_up)
    input_grad = lax.psum_scatter(
        input_terms.astype(jnp.bfloat16), "node", scatter_dimension=1, tiled=True
    )
    both_back = jnp.concatenate((gate_back, up_back), 1)
    first = contract_first(tokens, both_back)
    second = contract_first(cotangent, hidden)
    owned = lax.psum_scatter(
        (jnp.concatenate((first, second), 1) * grad_scale).astype(jnp.bfloat16),
        "local",
        scatter_dimension=0,
        tiled=True,
    ).astype(jnp.float32)
    gate_grad = owned[:, :unit_count]
    up_grad = owned[:, unit_count : 2 * unit_count]
    down_grad = owned[:, 2 * unit_count :].T
    return (block_out, input_grad, gate_grad, up_grad, down_grad)


def solution(mesh):
    placed = (
        P("local", None),
        P("local", None),
        P("local", "node"),
        P("local", "node"),
        P("node", "local"),
    )
    return jax.shard_map(
        per_device,
        mesh=mesh,
        in_specs=placed,
        out_specs=(
            P("local", "node"),
            P("local", "node"),
            P("local", "node"),
            P("local", "node"),
            P("node", "local"),
        ),
        check_vma=False,
    )
```

profile of v0, /device:TPU:0, one launch (start us, length us, event | category | flops | bytes accessed | tf_op | source)
XLA Modules:
  0.0 1492.8 jit_solution(17711385552550174454)
XLA Ops:
  7.2 0.0 all-gather.6.cloned.1.call-start
  7.2 0.7 all-gather.6.cloned.1.call-update
  7.9 0.0 all-gather.4.cloned.1.call-start
  7.9 0.7 all-gather.4.cloned.1.call-update
  8.6 0.0 all-gather.8.cloned.1.call-start
  8.7 0.7 all-gather.8.cloned.1.call-update
  9.4 0.0 reduce-scatter.8.cloned.1.call-start
  9.4 221.1 %all-gather.6.cloned.1.call-done = bf16[4096,1536]{1,0:T(8,128)(2,1)} async-done(((bf16[1024,1536]{1,0:T(8,128)(2,1)}), bf16[4096,1536]{1,0:T(8,128)(2,1)}) %all-gather.6.cloned.1.call-update) | async-done | bytes 12582928 | tf_op jit(solution)/shard_map/all_gather | solution.py:43
  230.5 12.0 fusion.8
  242.5 206.0 %all-gather.4.cloned.1.call-done = bf16[4096,1536]{1,0:T(8,128)(2,1)} async-done(((bf16[1024,1536]{1,0:T(8,128)(2,1)}), bf16[4096,1536]{1,0:T(8,128)(2,1)}) %all-gather.4.cloned.1.call-update) | async-done | bytes 12582928 | tf_op jit(solution)/shard_map/all_gather | solution.py:42
  448.5 12.0 fusion.7
  460.5 206.0 %all-gather.8.cloned.1.call-done = bf16[1536,4096]{1,0:T(8,128)(2,1)} async-done(((bf16[1536,1024]{1,0:T(8,128)(2,1)}), bf16[1536,4096]{1,0:T(8,128)(2,1)}) %all-gather.8.cloned.1.call-update) | async-done | bytes 12582928 | tf_op jit(solution)/shard_map/all_gather | solution.py:44
  666.5 16.2 %multiply_convert_fusion = (bf16[512,1536]{1,0:T(8,128)(2,1)S(1)}, bf16[512,1536]{1,0:T(8,128)(2,1)}, bf16[512,1536]{1,0:T(8,128)(2,1)S(1)}) fusion(f32[512,1536]{1,0:T(8,128)} %fusion.7, f32[512,1536]{1,0:T(8,128)} %fusion.8, bf16[512,4096]{1,0:T(8,128)(2,1)} %param.6, bf16[1536,4096]{1,0:T(8,128)(2,1)} %all-gather.8.cloned.1.call-done), kind=kOutput, calls=%fused_computation.10 | convolution fusion | flops 6454247424 | bytes 27787264 | tf_op jit(solution)/shard_map/dot_general | solution.py:25
  682.8 11.7 convolution_bitcast_fusion.1
  694.5 24.7 %convolution_bitcast_fusion = f32[4096,3072]{0,1:T(8,128)} fusion(bf16[512,4096]{1,0:T(8,128)(2,1)} %param.5, bf16[512,1536]{1,0:T(8,128)(2,1)S(1)} %get-tuple-element.12, bf16[512,1536]{1,0:T(8,128)(2,1)} %get-tuple-element.13), kind=kOutput, calls=%fused_computation.2 | convolution fusion | flops 12891193344 | bytes 57671680 | tf_op jit(solution)/shard_map/dot_general | solution.py:31
  719.2 37.5 %fusion = bf16[4096,4608]{0,1:T(8,128)(2,1)} fusion(f32[4096,1536]{0,1:T(8,128)} %convolution_bitcast_fusion.1, f32[4096,3072]{0,1:T(8,128)} %convolution_bitcast_fusion), kind=kLoop, calls=%fused_computation.1 | loop fusion | flops 56623104 | bytes 113246208 | tf_op jit(solution)/shard_map/convert_element_type | solution.py:63
  756.7 0.0 reduce-scatter.8.cloned.1.call-update
  756.7 0.0 reduce-scatter.6.cloned.1.call-start
  756.8 10.1 fusion.9
  766.9 12.8 add_convert_fusion
  779.8 0.0 reduce-scatter.6.cloned.1.call-update
  779.8 0.0 reduce-scatter.4.cloned.1.call-start
  779.8 13.1 convolution_convert_fusion
  793.0 0.0 reduce-scatter.4.cloned.1.call-update
  793.0 581.3 %reduce-scatter.8.cloned.1.call-done = bf16[1024,4608]{0,1:T(8,128)(2,1)} async-done(((bf16[4096,4608]{0,1:T(8,128)(2,1)}), bf16[1024,4608]{0,1:T(8,128)(2,1)}) %reduce-scatter.8.cloned.1.call-update) | async-done | bytes 9437200 | tf_op jit(solution)/shard_map/reduce_scatter | solution.py:62
  1374.3 9.1 fusion.6
  1383.4 6.9 copy.11
  1390.2 6.8 copy.10
  1397.0 12.6 convert_element_type.27
  1409.6 6.7 slice_bitcast_fusion
  1416.4 14.4 reduce-scatter.6.cloned.1.call-done
  1430.8 55.1 %reduce-scatter.4.cloned.1.call-done = bf16[512,512]{1,0:T(8,128)(2,1)} async-done(((bf16[512,4096]{1,0:T(8,128)(2,1)}), bf16[512,512]{1,0:T(8,128)(2,1)}) %reduce-scatter.4.cloned.1.call-update) | async-done | bytes 524304 | tf_op jit(solution)/shard_map/reduce_scatter | solution.py:50
  (2 shorter events, 0.0 us)
Async XLA Ops:
  7.2 223.3 %all-gather.6.cloned.1.call-start = ((), (), s32[]{:S(2)}) async-start(), calls=%async_computation.4 | async-start | bytes 15728640 | tf_op jit(solution)/shard_map/all_gather | solution.py:43
  7.9 440.6 %all-gather.4.cloned.1.call-start = ((), (), s32[]{:S(2)}) async-start(), calls=%async_computation.3 | async-start | bytes 15728640 | tf_op jit(solution)/shard_map/all_gather | solution.py:42
  8.6 657.9 %all-gather.8.cloned.1.call-start = ((), (), s32[]{:S(2)}) async-start(), calls=%async_computation.5 | async-start | bytes 15728640 | tf_op jit(solution)/shard_map/all_gather | solution.py:44
  9.4 1364.9 %reduce-scatter.8.cloned.1.call-start = ((), (), s32[]{:S(2)}) async-start(), calls=%async_computation.8 | async-start | bytes 47185920 | tf_op jit(solution)/shard_map/reduce_scatter | solution.py:62
  666.5 16.2 %copy-start = (bf16[512,4096]{1,0:T(8,128)(2,1)S(1)}, bf16[512,4096]{1,0:T(8,128)(2,1)}, u32[]{:S(2)}) copy-start(bf16[512,4096]{1,0:T(8,128)(2,1)} %param.6) | copy-start | bytes 12582916
  756.7 674.1 %reduce-scatter.6.cloned.1.call-start = ((), (), s32[]{:S(2)}) async-start(), calls=%async_computation.7 | async-start | bytes 4718592 | tf_op jit(solution)/shard_map/reduce_scatter | solution.py:56
  779.8 706.2 %reduce-scatter.4.cloned.1.call-start = ((), (), s32[]{:S(2)}) async-start(), calls=%async_computation.6 | async-start | bytes 4718592 | tf_op jit(solution)/shard_map/reduce_scatter | solution.py:50
Sparse Core Ops, SparseCore 0:
  9.6 220.8 all-gather.5
  232.1 216.3 all-gather.3
  450.1 216.3 all-gather.7
  756.8 617.3 reduce-scatter.7
  1378.4 52.3 reduce-scatter.5
  1434.6 51.3 reduce-scatter.3
where the time goes:
time: 1490 us
  waiting for transfers between devices  1290 us (87%)
  matrix products  113 us (8%)
  other arithmetic  50.1 us (3%)
  local copies, waits for them, and re-layouts  29.5 us (2%)
    reduce_scatter x1, waiting for transfers between devices, per_device(): lax.psum_scatter((jnp.concatenate((first, second), 1) * grad_scale).astyp...  581 us
    all_gather x1, waiting for transfers between devices, per_device(): lax.all_gather(up_weight, 'local', axis=0, tiled=True)  221 us
    all_gather x1, waiting for transfers between devices, per_device(): lax.all_gather(down_weight, 'local', axis=1, tiled=True)  206 us
    all_gather x1, waiting for transfers between devices, per_device(): lax.all_gather(gate_weight, 'local', axis=0, tiled=True)  206 us
    reduce_scatter x1, waiting for transfers between devices, per_device(): lax.psum_scatter(out_terms.astype(jnp.bfloat16), 'node', scatter_dimensio...  55.1 us
    dot_general x3, matrix products, contract_last(): lax.dot_general(left, right, (((1,), (1,)), ((), ())), preferred_element_...  39.2 us
    convert_element_type x1, other arithmetic, per_device(): (jnp.concatenate((first, second), 1) * grad_scale).astype(jnp.bfloat16)  37.5 us
    dot_general x2, matrix products, contract_first(): lax.dot_general(left, right, (((0,), (0,)), ((), ())), preferred_element_...  36.4 us
  transfers between devices with their start and end apart: 6, of which 6 were waited for; matrix products, arithmetic and copies ran while one was open for 7% of the time, Pallas kernels for 0%

commit v1 on v0

v1 whole, which is shorter than its diff:
```python
import math

import jax
import jax.numpy as jnp
from jax import lax
from jax.sharding import PartitionSpec as P

CHUNKS = 3


def dot_mid(left, right):
    return lax.dot_general(
        left, right, (((1,), (0,)), ((), ())), preferred_element_type=jnp.float32
    )


def contract_last(left, right):
    return lax.dot_general(
        left, right, (((1,), (1,)), ((), ())), preferred_element_type=jnp.float32
    )


def contract_first(left, right):
    return lax.dot_general(
        left, right, (((0,), (0,)), ((), ())), preferred_element_type=jnp.float32
    )


def gates(gate_part, up_part, hidden_back):
    sigma = jax.nn.sigmoid(gate_part)
    active = gate_part * sigma
    hidden = (active * up_part).astype(jnp.bfloat16)
    gate_back = (hidden_back * up_part * sigma * (1.0 + gate_part * (1.0 - sigma))).astype(
        jnp.bfloat16
    )
    up_back = (hidden_back * active).astype(jnp.bfloat16)
    return hidden, gate_back, up_back


def exchange(piece_for, groups, me):
    got = []
    for step in range(1, groups):
        pairs = [(i, (i + step) % groups) for i in range(groups)]
        piece = piece_for((me + step) % groups)
        got.append(((me - step) % groups, lax.ppermute(piece, "local", pairs)))
    got.append((me, piece_for(me)))
    return got


def per_device(tokens, cotangent, gate_weight, up_weight, down_weight):
    groups = lax.axis_size("local")
    nodes = lax.axis_size("node")
    me = lax.axis_index("local")
    node = lax.axis_index("node")
    rows, width = tokens.shape
    depth, unit_count = gate_weight.shape
    owned = unit_count // groups
    size = owned // CHUNKS
    grad_scale = 1.0 / math.sqrt(rows * groups)

    share = rows // nodes
    all_tok, all_cot = (
        lax.all_gather(
            lax.dynamic_slice_in_dim(a, node * share, share, 0),
            ("local", "node"),
            axis=0,
            tiled=True,
        )
        for a in (tokens, cotangent)
    )

    gate_grad = jnp.zeros((depth, unit_count), jnp.float32)
    up_grad = jnp.zeros((depth, unit_count), jnp.float32)
    down_grad = jnp.zeros((unit_count, depth), jnp.float32)
    weights = []
    for c in range(CHUNKS):
        gate = jnp.zeros((width, size), jnp.bfloat16)
        up = jnp.zeros((width, size), jnp.bfloat16)
        down = jnp.zeros((size, width), jnp.bfloat16)
        for src, p in exchange(
            lambda d: lax.dynamic_slice(gate_weight, (0, d * owned + c * size), (depth, size)),
            groups,
            me,
        ):
            gate = lax.dynamic_update_slice(gate, p, (src * depth, 0))
        for src, p in exchange(
            lambda d: lax.dynamic_slice(up_weight, (0, d * owned + c * size), (depth, size)),
            groups,
            me,
        ):
            up = lax.dynamic_update_slice(up, p, (src * depth, 0))
        for src, p in exchange(
            lambda d: lax.dynamic_slice(down_weight, (d * owned + c * size, 0), (size, depth)),
            groups,
            me,
        ):
            down = lax.dynamic_update_slice(down, p, (0, src * depth))
        weights.append((gate, up, down))

    kept = []
    for c, (gate, up, down) in enumerate(weights):
        gate_part = dot_mid(all_tok, gate)
        up_part = dot_mid(all_tok, up)
        hidden_back = contract_last(all_cot, down)
        hidden, gate_back, up_back = gates(gate_part, up_part, hidden_back)
        kept.append((hidden, gate_back, up_back))
        g_term, u_term, d_term = (
            (contract_first(all_tok, gate_back) * grad_scale).astype(jnp.bfloat16),
            (contract_first(all_tok, up_back) * grad_scale).astype(jnp.bfloat16),
            (contract_first(hidden, all_cot) * grad_scale).astype(jnp.bfloat16),
        )
        for src, p in exchange(
            lambda d: lax.dynamic_slice(g_term, (d * depth, 0), (depth, size)), groups, me
        ):
            gate_grad = lax.dynamic_update_slice(
                gate_grad, p.astype(jnp.float32), (0, src * owned + c * size)
            )
        for src, p in exchange(
            lambda d: lax.dynamic_slice(u_term, (d * depth, 0), (depth, size)), groups, me
        ):
            up_grad = lax.dynamic_update_slice(
                up_grad, p.astype(jnp.float32), (0, src * owned + c * size)
            )
        for src, p in exchange(
            lambda d: lax.dynamic_slice(d_term, (0, d * depth), (size, depth)), groups, me
        ):
            down_grad = lax.dynamic_update_slice(
                down_grad, p.astype(jnp.float32), (src * owned + c * size, 0)
            )

    hidden, gate_back, up_back = (jnp.concatenate(a, 1) for a in zip(*kept))
    gate, up = (jnp.concatenate([w[i] for w in weights], 1) for i in (0, 1))
    down = jnp.concatenate([w[2] for w in weights], 0)
    out_terms = dot_mid(hidden, down).astype(jnp.bfloat16)
    in_terms = (contract_last(gate_back, gate) + contract_last(up_back, up)).astype(jnp.bfloat16)

    def scatter(a):
        a = lax.psum_scatter(a, "node", scatter_dimension=1, tiled=True)
        return lax.psum_scatter(a, "local", scatter_dimension=0, tiled=True)

    return (scatter(out_terms), scatter(in_terms), gate_grad, up_grad, down_grad)


def solution(mesh):
    placed = (
        P("local", None),
        P("local", None),
        P("local", "node"),
        P("local", "node"),
        P("node", "local"),
    )
    return jax.shard_map(
        per_device,
        mesh=mesh,
        in_specs=placed,
        out_specs=(
            P("local", "node"),
            P("local", "node"),
            P("local", "node"),
            P("local", "node"),
            P("node", "local"),
        ),
        check_vma=False,
    )
```

time: 1490 us -> 879 us (0.59)
  waiting for transfers between devices: 1290 us -> 243 us
  starting transfers between devices: 0.24 us -> 285 us
  matrix products: 113 us -> 230 us
  local copies, waits for them, and re-layouts: 29.5 us -> 53 us
    reduce_scatter x3 -> x4, waiting for transfers between devices: 651 us -> 12.3 us  [the longest x2 7.01 us: scatter(): return lax.psum_scatter(a, 'local', scatter_dimension=0, tiled=True)]
    all_gather x3 -> x2, waiting for transfers between devices: 633 us -> 31.7 us  [per_device(): lax.all_gather(lax.dynamic_slice_in_dim(a, node * share, share, 0), ('loc...]
    ppermute x0 -> x54, starting transfers between devices: none -> 284 us  [exchange(): got.append(((me - step) % groups, lax.ppermute(piece, 'local', pairs)))]
    ppermute x0 -> x54, waiting for transfers between devices: none -> 199 us  [exchange(): got.append(((me - step) % groups, lax.ppermute(piece, 'local', pairs)))]
    dot_general x3 -> x7, matrix products: 37.1 us -> 93.5 us  [dot_mid(): lax.dot_general(left, right, (((1,), (0,)), ((), ())), preferred_element_...]
    convert_element_type x2 -> x0, other arithmetic: 50.1 us -> none  [the longest x1 37.5 us: per_device(): (jnp.concatenate((first, second), 1) * grad_scale).astype(jnp.bfloat16)]
    dynamic_update_slice x0 -> x36, other arithmetic: none -> 44.5 us  [the longest x12 17.7 us: per_device(): lax.dynamic_update_slice(gate_grad, p.astype(jnp.float32), (0, src * owne...]
    dot_general x3 -> x5, matrix products: 39.2 us -> 73.4 us  [contract_last(): lax.dot_general(left, right, (((1,), (1,)), ((), ())), preferred_element_...]
  transfers between devices with their start and end apart: 6 -> 60, of which waited for: 6 -> 23; matrix products, arithmetic and copies ran while one was open for 7% -> 26% of each run, Pallas kernels for 0% -> 0%
where the time goes in v1:
time: 879 us; the launch traced here: 871 us
  starting transfers between devices  285 us (32%)
  waiting for transfers between devices  243 us (28%)
  matrix products  230 us (26%)
  local copies, waits for them, and re-layouts  53 us (6%)
  other arithmetic  44.5 us (5%)
  between operations  15.6 us (2%)
    ppermute x54, starting transfers between devices, exchange(): got.append(((me - step) % groups, lax.ppermute(piece, 'local', pairs)))  284 us
    ppermute x54, waiting for transfers between devices, exchange(): got.append(((me - step) % groups, lax.ppermute(piece, 'local', pairs)))  199 us
    dot_general x7, matrix products, dot_mid(): lax.dot_general(left, right, (((1,), (0,)), ((), ())), preferred_element_...  93.5 us
    dot_general x5, matrix products, contract_last(): lax.dot_general(left, right, (((1,), (1,)), ((), ())), preferred_element_...  73.4 us
    dot_general x9, matrix products, contract_first(): lax.dot_general(left, right, (((0,), (0,)), ((), ())), preferred_element_...  62.8 us
    all_gather x2, waiting for transfers between devices, per_device(): lax.all_gather(lax.dynamic_slice_in_dim(a, node * share, share, 0), ('loc...  31.7 us
    dynamic_update_slice x12, other arithmetic, per_device(): lax.dynamic_update_slice(gate_grad, p.astype(jnp.float32), (0, src * owne...  17.7 us
  transfers between devices with their start and end apart: 60, of which 23 were waited for; matrix products, arithmetic and copies ran while one was open for 26% of the time, Pallas kernels for 0%

profile of v1, /device:TPU:0, one launch (start us, length us, event | category | flops | bytes accessed | tf_op | source)
XLA Modules:
  0.0 870.8 jit_solution(15709382477637438179)
XLA Ops:
  35.8 28.3 %collective-permute-start = (bf16[1024,128]{1,0:T(8,128)(2,1)}, bf16[1024,128]{1,0:T(8,128)(2,1)S(1)}, u32[]{:S(2)}, u32[]{:S(2)}) collective-permute-start(bf16[1024,128]{1,0:T(8,128)(2,1)} %get-tuple-element.14), channel_id=1, source_target_pairs={{0,1},{1,2},{2,3},{3,0},{4,5},{5,6},{6,7},{7,4},{8,9},{9,10},{10,1... | collective-permute-start | bytes 786440 | tf_op jit(solution)/shard_map/ppermute | solution.py:45
  66.3 28.2 %collective-permute-start.3 = (bf16[1024,128]{1,0:T(8,128)(2,1)}, bf16[1024,128]{1,0:T(8,128)(2,1)S(1)}, u32[]{:S(2)}, u32[]{:S(2)}) collective-permute-start(bf16[1024,128]{1,0:T(8,128)(2,1)} %get-tuple-element.24), channel_id=1, source_target_pairs={{0,1},{1,2},{2,3},{3,0},{4,5},{5,6},{6,7},{7,4},{8,9},{9,10},{10,1... | collective-permute-start | bytes 786440 | tf_op jit(solution)/shard_map/ppermute | solution.py:45
  105.6 14.7 %collective-permute-start.24 = (bf16[128,1024]{1,0:T(8,128)(2,1)S(1)}, bf16[128,1024]{1,0:T(8,128)(2,1)S(1)}, u32[]{:S(2)}, u32[]{:S(2)}) collective-permute-start(bf16[128,1024]{1,0:T(8,128)(2,1)S(1)} %get-tuple-element.31), channel_id=1, source_target_pairs={{0,1},{1,2},{2,3},{3,0},{4,5},{5,6},{6,7},{7,4},{8,9},{9,10},{10,1... | collective-permute-start | bytes 786440 | tf_op jit(solution)/shard_map/ppermute | solution.py:45
  120.5 11.0 %collective-permute-done.4 = bf16[1024,128]{1,0:T(8,128)(2,1)S(1)} collective-permute-done((bf16[1024,128]{1,0:T(8,128)(2,1)S(1)}, bf16[1024,128]{1,0:T(8,128)(2,1)S(1)}, u32[]{:S(2)}, u32[]{:S(2)}) %collective-permute-start.4) | collective-permute-done | bytes 262176 | tf_op jit(solution)/shard_map/ppermute | solution.py:45
  135.5 17.9 %collective-permute-start.26 = (bf16[128,1024]{1,0:T(8,128)(2,1)S(1)}, bf16[128,1024]{1,0:T(8,128)(2,1)S(1)}, u32[]{:S(2)}, u32[]{:S(2)}) collective-permute-start(bf16[128,1024]{1,0:T(8,128)(2,1)S(1)} %get-tuple-element.35), channel_id=1, source_target_pairs={{0,3},{1,0},{2,1},{3,2},{4,7},{5,4},{6,5},{7,6},{8,11},{9,8},{10,9... | collective-permute-start | bytes 786440 | tf_op jit(solution)/shard_map/ppermute | solution.py:45
  153.9 12.2 %collective-permute-start.13 = (bf16[1024,128]{1,0:T(8,128)(2,1)S(1)}, bf16[1024,128]{1,0:T(8,128)(2,1)S(1)}, u32[]{:S(2)}, u32[]{:S(2)}) collective-permute-start(bf16[1024,128]{1,0:T(8,128)(2,1)S(1)} %get-tuple-element.6), channel_id=1, source_target_pairs={{0,2},{1,3},{2,0},{3,1},{4,6},{5,7},{6,4},{7,5},{8,10},{9,11},{10,... | collective-permute-start | bytes 786440 | tf_op jit(solution)/shard_map/ppermute | solution.py:45
  166.3 44.5 %collective-permute-start.12 = (bf16[1024,128]{1,0:T(8,128)(2,1)S(1)}, bf16[1024,128]{1,0:T(8,128)(2,1)S(1)}, u32[]{:S(2)}, u32[]{:S(2)}) collective-permute-start(bf16[1024,128]{1,0:T(8,128)(2,1)S(1)} %get-tuple-element.7), channel_id=1, source_target_pairs={{0,1},{1,2},{2,3},{3,0},{4,5},{5,6},{6,7},{7,4},{8,9},{9,10},{10,1... | collective-permute-start | bytes 786440 | tf_op jit(solution)/shard_map/ppermute | solution.py:45
  215.1 17.2 %collective-permute-start.6 = (bf16[1024,128]{1,0:T(8,128)(2,1)S(1)}, bf16[1024,128]{1,0:T(8,128)(2,1)S(1)}, u32[]{:S(2)}, u32[]{:S(2)}) collective-permute-start(bf16[1024,128]{1,0:T(8,128)(2,1)S(1)} %get-tuple-element.10), channel_id=1, source_target_pairs={{0,1},{1,2},{2,3},{3,0},{4,5},{5,6},{6,7},{7,4},{8,9},{9,10},{10,1... | collective-permute-start | bytes 786440 | tf_op jit(solution)/shard_map/ppermute | solution.py:45
  238.4 9.4 %collective-permute-start.16 = (bf16[1024,128]{1,0:T(8,128)(2,1)S(1)}, bf16[1024,128]{1,0:T(8,128)(2,1)S(1)}, u32[]{:S(2)}, u32[]{:S(2)}) collective-permute-start(bf16[1024,128]{1,0:T(8,128)(2,1)S(1)} %get-tuple-element.16), channel_id=1, source_target_pairs={{0,2},{1,3},{2,0},{3,1},{4,6},{5,7},{6,4},{7,5},{8,10},{9,11},{10,... | collective-permute-start | bytes 786440 | tf_op jit(solution)/shard_map/ppermute | solution.py:45
  248.5 22.7 %collective-permute-start.15 = (bf16[1024,128]{1,0:T(8,128)(2,1)S(1)}, bf16[1024,128]{1,0:T(8,128)(2,1)S(1)}, u32[]{:S(2)}, u32[]{:S(2)}) collective-permute-start(bf16[1024,128]{1,0:T(8,128)(2,1)S(1)} %get-tuple-element.17), channel_id=1, source_target_pairs={{0,1},{1,2},{2,3},{3,0},{4,5},{5,6},{6,7},{7,4},{8,9},{9,10},{10,1... | collective-permute-start | bytes 786440 | tf_op jit(solution)/shard_map/ppermute | solution.py:45
  279.2 14.9 %collective-permute-start.17 = (bf16[1024,128]{1,0:T(8,128)(2,1)S(1)}, bf16[1024,128]{1,0:T(8,128)(2,1)S(1)}, u32[]{:S(2)}, u32[]{:S(2)}) collective-permute-start(bf16[1024,128]{1,0:T(8,128)(2,1)S(1)} %get-tuple-element.21), channel_id=1, source_target_pairs={{0,3},{1,0},{2,1},{3,2},{4,7},{5,4},{6,5},{7,6},{8,11},{9,8},{10,9... | collective-permute-start | bytes 786440 | tf_op jit(solution)/shard_map/ppermute | solution.py:45
  294.5 13.9 %collective-permute-done.9 = bf16[1024,128]{1,0:T(8,128)(2,1)S(1)} collective-permute-done((bf16[1024,128]{1,0:T(8,128)(2,1)S(1)}, bf16[1024,128]{1,0:T(8,128)(2,1)S(1)}, u32[]{:S(2)}, u32[]{:S(2)}) %collective-permute-start.9) | collective-permute-done | bytes 262176 | tf_op jit(solution)/shard_map/ppermute | solution.py:45
  308.6 19.7 %collective-permute-done.10 = bf16[1024,128]{1,0:T(8,128)(2,1)S(1)} collective-permute-done((bf16[1024,128]{1,0:T(8,128)(2,1)S(1)}, bf16[1024,128]{1,0:T(8,128)(2,1)S(1)}, u32[]{:S(2)}, u32[]{:S(2)}) %collective-permute-start.10) | collective-permute-done | bytes 262176 | tf_op jit(solution)/shard_map/ppermute | solution.py:45
  331.2 13.2 %fusion.50 = f32[2048,128]{0,1:T(8,128)} fusion(bf16[2048,4096]{1,0:T(8,128)(2,1)} %all-gather.5.cloned.1.call-done, bf16[128,4096]{1,0:T(8,128)(2,1)} %copy-done.15), kind=kOutput, calls=%fused_computation.201 | convolution fusion | flops 2147483648 | bytes 18874368 | tf_op jit(solution)/shard_map/dot_general | solution.py:18
  358.5 31.7 %all-gather.3.cloned.1.call-done = bf16[2048,4096]{1,0:T(8,128)(2,1)} async-done(((bf16[64,4096]{1,0:T(8,128)(2,1)}), bf16[2048,4096]{1,0:T(8,128)(2,1)}) %all-gather.3.cloned.1.call-update) | async-done | bytes 16777232 | tf_op jit(solution)/shard_map/all_gather | solution.py:63
  390.3 12.4 %fusion.47 = f32[2048,128]{0,1:T(8,128)} fusion(bf16[2048,4096]{1,0:T(8,128)(2,1)} %all-gather.3.cloned.1.call-done, bf16[4096,128]{1,0:T(8,128)(2,1)S(1)} %get-tuple-element.27), kind=kOutput, calls=%fused_computation.198 | convolution fusion | flops 2147483648 | bytes 18874368 | tf_op jit(solution)/shard_map/dot_general | solution.py:12
  402.7 12.4 %fusion.48 = f32[2048,128]{0,1:T(8,128)} fusion(bf16[2048,4096]{1,0:T(8,128)(2,1)} %all-gather.3.cloned.1.call-done, bf16[4096,128]{1,0:T(8,128)(2,1)S(1)} %get-tuple-element.28), kind=kOutput, calls=%fused_computation.199 | convolution fusion | flops 2147483648 | bytes 18874368 | tf_op jit(solution)/shard_map/dot_general | solution.py:12
  415.1 12.6 %fusion.46 = f32[2048,128]{0,1:T(8,128)} fusion(bf16[2048,4096]{1,0:T(8,128)(2,1)} %all-gather.3.cloned.1.call-done, bf16[4096,128]{1,0:T(8,128)(2,1)S(1)} %get-tuple-element.15), kind=kOutput, calls=%fused_computation.197 | convolution fusion | flops 2147483648 | bytes 18874368 | tf_op jit(solution)/shard_map/dot_general | solution.py:12
  427.7 13.8 %multiply_convert_fusion.4 = (bf16[2048,128]{0,1:T(8,128)(2,1)}, bf16[2048,128]{0,1:T(8,128)(2,1)}, bf16[2048,128]{0,1:T(8,128)(2,1)}) fusion(f32[2048,128]{0,1:T(8,128)} %fusion.50, f32[2048,128]{0,1:T(8,128)} %fusion.47, bf16[2048,4096]{1,0:T(8,128)(2,1)} %all-gather.3.cloned.1.call-done, bf16[4096,128]{1,0:T(8,128)(2,1)} %get-tuple-element.25), kind=kOutput, calls=%fused_computation.55 | convolution fusion | flops 2151415808 | bytes 21495808 | tf_op jit(solution)/shard_map/dot_general | solution.py:12
  441.5 13.8 %multiply_convert_fusion.3 = (bf16[2048,128]{0,1:T(8,128)(2,1)}, bf16[2048,128]{0,1:T(8,128)(2,1)}, bf16[2048,128]{0,1:T(8,128)(2,1)}) fusion(f32[2048,128]{0,1:T(8,128)} %fusion.51, f32[2048,128]{0,1:T(8,128)} %fusion.48, bf16[2048,4096]{1,0:T(8,128)(2,1)} %all-gather.3.cloned.1.call-done, bf16[4096,128]{1,0:T(8,128)(2,1)} %get-tuple-element.26), kind=kOutput, calls=%fused_computation.54 | convolution fusion | flops 2151415808 | bytes 21495808 | tf_op jit(solution)/shard_map/dot_general | solution.py:12
  455.3 14.2 %multiply_convert_fusion.5 = (bf16[2048,128]{0,1:T(8,128)(2,1)}, bf16[2048,128]{0,1:T(8,128)(2,1)}, bf16[2048,128]{0,1:T(8,128)(2,1)}) fusion(f32[2048,128]{0,1:T(8,128)} %fusion.49, f32[2048,128]{0,1:T(8,128)} %fusion.46, bf16[2048,4096]{1,0:T(8,128)(2,1)} %all-gather.3.cloned.1.call-done, bf16[4096,128]{1,0:T(8,128)(2,1)} %copy-done.1), kind=kOutput, calls=%fused_computation.56 | convolution fusion | flops 2151415808 | bytes 21495808 | tf_op jit(solution)/shard_map/dot_general | solution.py:12
  469.4 14.3 %convolution_convert_fusion = bf16[2048,4096]{1,0:T(8,128)(2,1)} fusion(bf16[128,4096]{1,0:T(8,128)(2,1)} %copy-done.13, bf16[128,4096]{1,0:T(8,128)(2,1)} %copy-done.15, bf16[128,4096]{1,0:T(8,128)(2,1)} %copy-done.11, bf16[2048,128]{0,1:T(8,128)(2,1)} %get-tuple-element.49, bf16[2048,128]{0,1:T(8,128)(2,1)} %get-tuple-element.46, ...), kind=kOutput, calls=%fused_computation.1 | convolution fusion | flops 6464995328 | bytes 21495808 | tf_op jit(solution)/shard_map/dot_general | solution.py:12
  483.9 23.4 %fusion.19 = f32[2048,4096]{1,0:T(8,128)} fusion(bf16[4096,128]{1,0:T(8,128)(2,1)S(1)} %get-tuple-element.28, bf16[4096,128]{1,0:T(8,128)(2,1)S(1)} %get-tuple-element.27, bf16[4096,128]{1,0:T(8,128)(2,1)S(1)} %get-tuple-element.15, bf16[2048,128]{0,1:T(8,128)(2,1)} %get-tuple-element.48, bf16[2048,128]{0,1:T(8,128)(2,1)} %get-tuple-element.45, ...), kind=kOutput, calls=%fused_computation.30 | convolution fusion | flops 6456606720 | bytes 38273024 | tf_op jit(solution)/shard_map/dot_general | solution.py:18
  507.3 23.2 %add_convert_fusion = bf16[2048,4096]{1,0:T(8,128)(2,1)} fusion(f32[2048,4096]{1,0:T(8,128)} %fusion.19, bf16[4096,128]{1,0:T(8,128)(2,1)} %get-tuple-element.26, bf16[4096,128]{1,0:T(8,128)(2,1)} %get-tuple-element.25, bf16[4096,128]{1,0:T(8,128)(2,1)} %copy-done.1, bf16[2048,128]{0,1:T(8,128)(2,1)} %get-tuple-element.47, ...), kind=kOutput, calls=%fused_computation | convolution fusion | flops 6473383936 | bytes 55050240 | tf_op jit(solution)/shard_map/dot_general | solution.py:18
  531.5 9.0 %fusion.1 = bf16[4096,128]{1,0:T(8,128)(2,1)S(1)} fusion(bf16[2048,4096]{1,0:T(8,128)(2,1)} %all-gather.3.cloned.1.call-done, bf16[2048,128]{0,1:T(8,128)(2,1)S(1)} %copy-done.20), kind=kOutput, calls=%fused_computation.12 | convolution fusion | flops 2148532224 | bytes 18350080 | tf_op jit(solution)/shard_map/dot_general | solution.py:24
  564.5 8.8 %fusion.4 = bf16[4096,128]{1,0:T(8,128)(2,1)S(1)} fusion(bf16[2048,4096]{1,0:T(8,128)(2,1)} %all-gather.3.cloned.1.call-done, bf16[2048,128]{0,1:T(8,128)(2,1)S(1)} %copy-done.23), kind=kOutput, calls=%fused_computation.15 | convolution fusion | flops 2148532224 | bytes 18350080 | tf_op jit(solution)/shard_map/dot_general | solution.py:24
  577.8 9.2 %fusion.2 = bf16[4096,128]{1,0:T(8,128)(2,1)S(1)} fusion(bf16[2048,4096]{1,0:T(8,128)(2,1)} %all-gather.3.cloned.1.call-done, bf16[2048,128]{0,1:T(8,128)(2,1)S(1)} %copy-done.18), kind=kOutput, calls=%fused_computation.13 | convolution fusion | flops 2148532224 | bytes 18350080 | tf_op jit(solution)/shard_map/dot_general | solution.py:24
  601.9 9.1 %fusion.8 = bf16[128,4096]{1,0:T(8,128)(2,1)S(1)} fusion(bf16[2048,128]{0,1:T(8,128)(2,1)} %get-tuple-element.49, bf16[2048,4096]{1,0:T(8,128)(2,1)} %all-gather.5.cloned.1.call-done), kind=kOutput, calls=%fused_computation.19 | convolution fusion | flops 2148532224 | bytes 18350080 | tf_op jit(solution)/shard_map/dot_general | solution.py:24
  682.4 15.2 %collective-permute-done.49 = bf16[128,1024]{1,0:T(8,128)(2,1)S(1)} collective-permute-done((bf16[128,1024]{1,0:T(8,128)(2,1)S(1)}, bf16[128,1024]{1,0:T(8,128)(2,1)S(1)}, u32[]{:S(2)}, u32[]{:S(2)}) %collective-permute-start.49) | collective-permute-done | bytes 262176 | tf_op jit(solution)/shard_map/ppermute | solution.py:45
  734.3 36.6 %collective-permute-done.52 = bf16[128,1024]{1,0:T(8,128)(2,1)S(1)} collective-permute-done((bf16[128,1024]{1,0:T(8,128)(2,1)}, bf16[128,1024]{1,0:T(8,128)(2,1)S(1)}, u32[]{:S(2)}, u32[]{:S(2)}) %collective-permute-start.52) | collective-permute-done | bytes 262176 | tf_op jit(solution)/shard_map/ppermute | solution.py:45
  776.1 13.4 %collective-permute-done.37 = bf16[1024,128]{1,0:T(8,128)(2,1)S(1)} collective-permute-done((bf16[1024,128]{1,0:T(8,128)(2,1)}, bf16[1024,128]{1,0:T(8,128)(2,1)S(1)}, u32[]{:S(2)}, u32[]{:S(2)}) %collective-permute-start.37) | collective-permute-done | bytes 262176 | tf_op jit(solution)/shard_map/ppermute | solution.py:45
  814.0 34.7 %collective-permute-done.53 = bf16[128,1024]{1,0:T(8,128)(2,1)S(1)} collective-permute-done((bf16[128,1024]{1,0:T(8,128)(2,1)S(1)}, bf16[128,1024]{1,0:T(8,128)(2,1)S(1)}, u32[]{:S(2)}, u32[]{:S(2)}) %collective-permute-start.53) | collective-permute-done | bytes 262176 | tf_op jit(solution)/shard_map/ppermute | solution.py:45
  (310 shorter events, 279.4 us)
Async XLA Ops:
  7.2 324.0 %all-gather.5.cloned.1.call-start = ((), (), s32[]{:S(2)}) async-start(), calls=%async_computation.7 | async-start | bytes 17301504 | tf_op jit(solution)/shard_map/all_gather | solution.py:63
  9.3 381.0 %all-gather.3.cloned.1.call-start = ((), (), s32[]{:S(2)}) async-start(), calls=%async_computation.4 | async-start | bytes 17301504 | tf_op jit(solution)/shard_map/all_gather | solution.py:63
  11.2 590.3 %reduce-scatter.5.cloned.1.call-start = ((), (), s32[]{:S(2)}) async-start(), calls=%async_computation.5 | async-start | bytes 18874368 | tf_op jit(solution)/shard_map/reduce_scatter | solution.py:138
  13.3 51.8 %collective-permute-start.19 = (bf16[128,1024]{1,0:T(8,128)(2,1)}, bf16[128,1024]{1,0:T(8,128)(2,1)}, u32[]{:S(2)}, u32[]{:S(2)}) collective-permute-start(bf16[128,1024]{1,0:T(8,128)(2,1)} %get-tuple-element.37), channel_id=1, source_target_pairs={{0,2},{1,3},{2,0},{3,1},{4,6},{5,7},{6,4},{7,5},{8,10},{9,11},{10,... | collective-permute-start | bytes 786440 | tf_op jit(solution)/shard_map/ppermute | solution.py:45
  20.9 110.6 %collective-permute-start.2 = (bf16[1024,128]{1,0:T(8,128)(2,1)S(1)}, bf16[1024,128]{1,0:T(8,128)(2,1)}, u32[]{:S(2)}, u32[]{:S(2)}) collective-permute-start(bf16[1024,128]{1,0:T(8,128)(2,1)S(1)} %get-tuple-element.12), channel_id=1, source_target_pairs={{0,3},{1,0},{2,1},{3,2},{4,7},{5,4},{6,5},{7,6},{8,11},{9,8},{10,9... | collective-permute-start | bytes 786440 | tf_op jit(solution)/shard_map/ppermute | solution.py:45
  23.2 76.9 %collective-permute-start.1 = (bf16[1024,128]{1,0:T(8,128)(2,1)}, bf16[1024,128]{1,0:T(8,128)(2,1)}, u32[]{:S(2)}, u32[]{:S(2)}) collective-permute-start(bf16[1024,128]{1,0:T(8,128)(2,1)} %get-tuple-element.13), channel_id=1, source_target_pairs={{0,2},{1,3},{2,0},{3,1},{4,6},{5,7},{6,4},{7,5},{8,10},{9,11},{10,... | collective-permute-start | bytes 786440 | tf_op jit(solution)/shard_map/ppermute | solution.py:45
  35.8 59.9 %collective-permute-start = (bf16[1024,128]{1,0:T(8,128)(2,1)}, bf16[1024,128]{1,0:T(8,128)(2,1)S(1)}, u32[]{:S(2)}, u32[]{:S(2)}) collective-permute-start(bf16[1024,128]{1,0:T(8,128)(2,1)} %get-tuple-element.14), channel_id=1, source_target_pairs={{0,1},{1,2},{2,3},{3,0},{4,5},{5,6},{6,7},{7,4},{8,9},{9,10},{10,1... | collective-permute-start | bytes 786440 | tf_op jit(solution)/shard_map/ppermute | solution.py:45
  65.2 66.5 %collective-permute-start.5 = (bf16[1024,128]{1,0:T(8,128)(2,1)}, bf16[1024,128]{1,0:T(8,128)(2,1)S(1)}, u32[]{:S(2)}, u32[]{:S(2)}) collective-permute-start(bf16[1024,128]{1,0:T(8,128)(2,1)} %get-tuple-element.22), channel_id=1, source_target_pairs={{0,3},{1,0},{2,1},{3,2},{4,7},{5,4},{6,5},{7,6},{8,11},{9,8},{10,9... | collective-permute-start | bytes 786440 | tf_op jit(solution)/shard_map/ppermute | solution.py:45
  100.1 53.8 %collective-permute-start.25 = (bf16[128,1024]{1,0:T(8,128)(2,1)S(1)}, bf16[128,1024]{1,0:T(8,128)(2,1)S(1)}, u32[]{:S(2)}, u32[]{:S(2)}) collective-permute-start(bf16[128,1024]{1,0:T(8,128)(2,1)S(1)} %get-tuple-element.30), channel_id=1, source_target_pairs={{0,2},{1,3},{2,0},{3,1},{4,6},{5,7},{6,4},{7,5},{8,10},{9,11},{10,... | collective-permute-start | bytes 786440 | tf_op jit(solution)/shard_map/ppermute | solution.py:45
  131.5 79.5 %collective-permute-start.23 = (bf16[128,1024]{1,0:T(8,128)(2,1)S(1)}, bf16[128,1024]{1,0:T(8,128)(2,1)S(1)}, u32[]{:S(2)}, u32[]{:S(2)}) collective-permute-start(bf16[128,1024]{1,0:T(8,128)(2,1)S(1)} %get-tuple-element.32), channel_id=1, source_target_pairs={{0,3},{1,0},{2,1},{3,2},{4,7},{5,4},{6,5},{7,6},{8,11},{9,8},{10,9... | collective-permute-start | bytes 786440 | tf_op jit(solution)/shard_map/ppermute | solution.py:45
  131.6 79.4 %collective-permute-start.22 = (bf16[128,1024]{1,0:T(8,128)(2,1)S(1)}, bf16[128,1024]{1,0:T(8,128)(2,1)S(1)}, u32[]{:S(2)}, u32[]{:S(2)}) collective-permute-start(bf16[128,1024]{1,0:T(8,128)(2,1)S(1)} %get-tuple-element.33), channel_id=1, source_target_pairs={{0,2},{1,3},{2,0},{3,1},{4,6},{5,7},{6,4},{7,5},{8,10},{9,11},{10,... | collective-permute-start | bytes 786440 | tf_op jit(solution)/shard_map/ppermute | solution.py:45
  135.5 79.5 %collective-permute-start.26 = (bf16[128,1024]{1,0:T(8,128)(2,1)S(1)}, bf16[128,1024]{1,0:T(8,128)(2,1)S(1)}, u32[]{:S(2)}, u32[]{:S(2)}) collective-permute-start(bf16[128,1024]{1,0:T(8,128)(2,1)S(1)} %get-tuple-element.35), channel_id=1, source_target_pairs={{0,3},{1,0},{2,1},{3,2},{4,7},{5,4},{6,5},{7,6},{8,11},{9,8},{10,9... | collective-permute-start | bytes 786440 | tf_op jit(solution)/shard_map/ppermute | solution.py:45
  153.9 84.5 %collective-permute-start.13 = (bf16[1024,128]{1,0:T(8,128)(2,1)S(1)}, bf16[1024,128]{1,0:T(8,128)(2,1)S(1)}, u32[]{:S(2)}, u32[]{:S(2)}) collective-permute-start(bf16[1024,128]{1,0:T(8,128)(2,1)S(1)} %get-tuple-element.6), channel_id=1, source_target_pairs={{0,2},{1,3},{2,0},{3,1},{4,6},{5,7},{6,4},{7,5},{8,10},{9,11},{10,... | collective-permute-start | bytes 786440 | tf_op jit(solution)/shard_map/ppermute | solution.py:45
  166.3 66.1 %collective-permute-start.12 = (bf16[1024,128]{1,0:T(8,128)(2,1)S(1)}, bf16[1024,128]{1,0:T(8,128)(2,1)S(1)}, u32[]{:S(2)}, u32[]{:S(2)}) collective-permute-start(bf16[1024,128]{1,0:T(8,128)(2,1)S(1)} %get-tuple-element.7), channel_id=1, source_target_pairs={{0,1},{1,2},{2,3},{3,0},{4,5},{5,6},{6,7},{7,4},{8,9},{9,10},{10,1... | collective-permute-start | bytes 786440 | tf_op jit(solution)/shard_map/ppermute | solution.py:45
  211.0 62.8 %collective-permute-start.8 = (bf16[1024,128]{1,0:T(8,128)(2,1)S(1)}, bf16[1024,128]{1,0:T(8,128)(2,1)S(1)}, u32[]{:S(2)}, u32[]{:S(2)}) collective-permute-start(bf16[1024,128]{1,0:T(8,128)(2,1)S(1)} %get-tuple-element.8), channel_id=1, source_target_pairs={{0,3},{1,0},{2,1},{3,2},{4,7},{5,4},{6,5},{7,6},{8,11},{9,8},{10,9... | collective-permute-start | bytes 786440 | tf_op jit(solution)/shard_map/ppermute | solution.py:45
  211.1 61.9 %collective-permute-start.7 = (bf16[1024,128]{1,0:T(8,128)(2,1)S(1)}, bf16[1024,128]{1,0:T(8,128)(2,1)S(1)}, u32[]{:S(2)}, u32[]{:S(2)}) collective-permute-start(bf16[1024,128]{1,0:T(8,128)(2,1)S(1)} %get-tuple-element.9), channel_id=1, source_target_pairs={{0,2},{1,3},{2,0},{3,1},{4,6},{5,7},{6,4},{7,5},{8,10},{9,11},{10,... | collective-permute-start | bytes 786440 | tf_op jit(solution)/shard_map/ppermute | solution.py:45
  238.4 56.1 %collective-permute-start.16 = (bf16[1024,128]{1,0:T(8,128)(2,1)S(1)}, bf16[1024,128]{1,0:T(8,128)(2,1)S(1)}, u32[]{:S(2)}, u32[]{:S(2)}) collective-permute-start(bf16[1024,128]{1,0:T(8,128)(2,1)S(1)} %get-tuple-element.16), channel_id=1, source_target_pairs={{0,2},{1,3},{2,0},{3,1},{4,6},{5,7},{6,4},{7,5},{8,10},{9,11},{10,... | collective-permute-start | bytes 786440 | tf_op jit(solution)/shard_map/ppermute | solution.py:45
  273.0 55.4 %collective-permute-start.11 = (bf16[1024,128]{1,0:T(8,128)(2,1)S(1)}, bf16[1024,128]{1,0:T(8,128)(2,1)S(1)}, u32[]{:S(2)}, u32[]{:S(2)}) collective-permute-start(bf16[1024,128]{1,0:T(8,128)(2,1)S(1)} %get-tuple-element.18), channel_id=1, source_target_pairs={{0,3},{1,0},{2,1},{3,2},{4,7},{5,4},{6,5},{7,6},{8,11},{9,8},{10,9... | collective-permute-start | bytes 786440 | tf_op jit(solution)/shard_map/ppermute | solution.py:45
  273.7 54.6 %collective-permute-start.10 = (bf16[1024,128]{1,0:T(8,128)(2,1)S(1)}, bf16[1024,128]{1,0:T(8,128)(2,1)S(1)}, u32[]{:S(2)}, u32[]{:S(2)}) collective-permute-start(bf16[1024,128]{1,0:T(8,128)(2,1)S(1)} %get-tuple-element.19), channel_id=1, source_target_pairs={{0,2},{1,3},{2,0},{3,1},{4,6},{5,7},{6,4},{7,5},{8,10},{9,11},{10,... | collective-permute-start | bytes 786440 | tf_op jit(solution)/shard_map/ppermute | solution.py:45
  279.2 49.2 %collective-permute-start.17 = (bf16[1024,128]{1,0:T(8,128)(2,1)S(1)}, bf16[1024,128]{1,0:T(8,128)(2,1)S(1)}, u32[]{:S(2)}, u32[]{:S(2)}) collective-permute-start(bf16[1024,128]{1,0:T(8,128)(2,1)S(1)} %get-tuple-element.21), channel_id=1, source_target_pairs={{0,3},{1,0},{2,1},{3,2},{4,7},{5,4},{6,5},{7,6},{8,11},{9,8},{10,9... | collective-permute-start | bytes 786440 | tf_op jit(solution)/shard_map/ppermute | solution.py:45
  483.8 233.8 %reduce-scatter.9.cloned.1.call-start = ((), (), s32[]{:S(2)}) async-start(), calls=%async_computation.8 | async-start | bytes 18874368 | tf_op jit(solution)/shard_map/reduce_scatter | solution.py:138
  530.5 325.9 %reduce-scatter.7.cloned.1.call-start = ((), (), s32[]{:S(2)}) async-start(), calls=%async_computation.6 | async-start | bytes 2621440 | tf_op jit(solution)/shard_map/reduce_scatter | solution.py:139
  542.5 156.0 %collective-permute-start.32 = (bf16[1024,128]{1,0:T(8,128)(2,1)}, bf16[1024,128]{1,0:T(8,128)(2,1)}, u32[]{:S(2)}, u32[]{:S(2)}) collective-permute-start(bf16[1024,128]{1,0:T(8,128)(2,1)} %get-tuple-element.71), channel_id=1, source_target_pairs={{0,3},{1,0},{2,1},{3,2},{4,7},{5,4},{6,5},{7,6},{8,11},{9,8},{10,9... | collective-permute-start | bytes 786440 | tf_op jit(solution)/shard_map/ppermute | solution.py:45
  544.6 136.0 %collective-permute-start.31 = (bf16[1024,128]{1,0:T(8,128)(2,1)}, bf16[1024,128]{1,0:T(8,128)(2,1)}, u32[]{:S(2)}, u32[]{:S(2)}) collective-permute-start(bf16[1024,128]{1,0:T(8,128)(2,1)} %get-tuple-element.72), channel_id=1, source_target_pairs={{0,2},{1,3},{2,0},{3,1},{4,6},{5,7},{6,4},{7,5},{8,10},{9,11},{10,... | collective-permute-start | bytes 786440 | tf_op jit(solution)/shard_map/ppermute | solution.py:45
  545.0 115.4 %collective-permute-start.30 = (bf16[1024,128]{1,0:T(8,128)(2,1)}, bf16[1024,128]{1,0:T(8,128)(2,1)}, u32[]{:S(2)}, u32[]{:S(2)}) collective-permute-start(bf16[1024,128]{1,0:T(8,128)(2,1)} %get-tuple-element.73), channel_id=1, source_target_pairs={{0,1},{1,2},{2,3},{3,0},{4,5},{5,6},{6,7},{7,4},{8,9},{9,10},{10,1... | collective-permute-start | bytes 786440 | tf_op jit(solution)/shard_map/ppermute | solution.py:45
  556.3 65.7 %collective-permute-start.45 = (bf16[128,1024]{1,0:T(8,128)(2,1)}, bf16[128,1024]{1,0:T(8,128)(2,1)}, u32[]{:S(2)}, u32[]{:S(2)}) collective-permute-start(bf16[128,1024]{1,0:T(8,128)(2,1)} %get-tuple-element.58), channel_id=1, source_target_pairs={{0,1},{1,2},{2,3},{3,0},{4,5},{5,6},{6,7},{7,4},{8,9},{9,10},{10,1... | collective-permute-start | bytes 786440 | tf_op jit(solution)/shard_map/ppermute | solution.py:45
  601.6 261.9 %reduce-scatter.11.cloned.1.call-start = ((), (), s32[]{:S(2)}) async-start(), calls=%async_computation.9 | async-start | bytes 2621440 | tf_op jit(solution)/shard_map/reduce_scatter | solution.py:139
  638.9 168.3 %collective-permute-start.41 = (bf16[1024,128]{1,0:T(8,128)(2,1)}, bf16[1024,128]{1,0:T(8,128)(2,1)}, u32[]{:S(2)}, u32[]{:S(2)}) collective-permute-start(bf16[1024,128]{1,0:T(8,128)(2,1)} %get-tuple-element.62), channel_id=1, source_target_pairs={{0,3},{1,0},{2,1},{3,2},{4,7},{5,4},{6,5},{7,6},{8,11},{9,8},{10,9... | collective-permute-start | bytes 786440 | tf_op jit(solution)/shard_map/ppermute | solution.py:45
  658.3 145.1 %collective-permute-start.40 = (bf16[1024,128]{1,0:T(8,128)(2,1)}, bf16[1024,128]{1,0:T(8,128)(2,1)}, u32[]{:S(2)}, u32[]{:S(2)}) collective-permute-start(bf16[1024,128]{1,0:T(8,128)(2,1)} %get-tuple-element.63), channel_id=1, source_target_pairs={{0,2},{1,3},{2,0},{3,1},{4,6},{5,7},{6,4},{7,5},{8,10},{9,11},{10,... | collective-permute-start | bytes 786440 | tf_op jit(solution)/shard_map/ppermute | solution.py:45
  680.6 120.9 %collective-permute-start.39 = (bf16[1024,128]{1,0:T(8,128)(2,1)}, bf16[1024,128]{1,0:T(8,128)(2,1)}, u32[]{:S(2)}, u32[]{:S(2)}) collective-permute-start(bf16[1024,128]{1,0:T(8,128)(2,1)} %get-tuple-element.64), channel_id=1, source_target_pairs={{0,1},{1,2},{2,3},{3,0},{4,5},{5,6},{6,7},{7,4},{8,9},{9,10},{10,1... | collective-permute-start | bytes 786440 | tf_op jit(solution)/shard_map/ppermute | solution.py:45
  798.9 54.9 %collective-permute-start.44 = (bf16[1024,128]{1,0:T(8,128)(2,1)S(1)}, bf16[1024,128]{1,0:T(8,128)(2,1)S(1)}, u32[]{:S(2)}, u32[]{:S(2)}) collective-permute-start(bf16[1024,128]{1,0:T(8,128)(2,1)S(1)} %get-tuple-element.59), channel_id=1, source_target_pairs={{0,3},{1,0},{2,1},{3,2},{4,7},{5,4},{6,5},{7,6},{8,11},{9,8},{10,9... | collective-permute-start | bytes 786440 | tf_op jit(solution)/shard_map/ppermute | solution.py:45
  801.6 51.4 %collective-permute-start.43 = (bf16[1024,128]{1,0:T(8,128)(2,1)S(1)}, bf16[1024,128]{1,0:T(8,128)(2,1)S(1)}, u32[]{:S(2)}, u32[]{:S(2)}) collective-permute-start(bf16[1024,128]{1,0:T(8,128)(2,1)S(1)} %copy-done.24), channel_id=1, source_target_pairs={{0,2},{1,3},{2,0},{3,1},{4,6},{5,7},{6,4},{7,5},{8,10},{9,11},{10,... | collective-permute-start | bytes 786440 | tf_op jit(solution)/shard_map/ppermute | solution.py:45
  (77 other events, 2087.0 us)
Sparse Core Ops, SparseCore 0:
  11.4 224.8 all-gather.4
  239.8 150.4 all-gather.2
  483.9 114.1 reduce-scatter.4
  601.5 116.0 reduce-scatter.8
  720.3 73.8 reduce-scatter.6
  797.0 66.4 reduce-scatter.10

commit v2 on v0

v2 whole, which is shorter than its diff:
```python
import math

import jax
import jax.numpy as jnp
from jax import lax
from jax.sharding import PartitionSpec as P


def dot(left, right, dims):
    return lax.dot_general(left, right, (dims, ((), ())), preferred_element_type=jnp.float32)


def after(value, *others):
    return lax.optimization_barrier((value, *others))[0]


def shift(value, step, groups):
    return lax.ppermute(value, "local", [(i, (i + step) % groups) for i in range(groups)])


def up_line(value, senders):
    return lax.ppermute(value, "local", [(i, i + 1) for i in senders])


def down_line(value, senders):
    return lax.ppermute(value, "local", [(i, i - 1) for i in senders])


def shift_order(groups):
    return sorted(range(1, groups), key=lambda k: -min(k, groups - k))


def add(a, b):
    return (a.astype(jnp.float32) + b.astype(jnp.float32)).astype(jnp.bfloat16)


def swap(value, bit, nodes):
    return lax.ppermute(value, "node", [(i, i ^ bit) for i in range(nodes)])


NEAR = (0, 2, 6, 4)


def node_sum(sent, kept, nodes, waits):
    half, f = sent.shape[0] // 2, sent.shape[1] // 4
    came = swap(sent, 1, nodes)

    def part(low, high, first):
        at = (slice(0, half) if first else slice(half, None), slice(low * f, high * f))
        return add(kept[at], came[at])

    one_in, two_in = after((part(1, 3, True), part(2, 4, False)), *waits)
    one_in, two_in = swap(one_in, 2, nodes), swap(two_in, 4, nodes)
    one_out = swap(add(part(3, 4, True), one_in[:, f:]), 4, nodes)
    two_out = swap(add(part(1, 2, False), two_in[:, :f]), 2, nodes)
    one = add(add(part(0, 1, True), one_in[:, :f]), one_out)
    two = add(add(part(0, 1, False), two_in[:, f:]), two_out)
    return (one, two), (one_in, two_in)


def line_sum(terms, groups, waits):
    up = down = None
    for step in range(1, groups):
        up_out, down_out = terms[step], terms[groups - step]
        if step > 1:
            up_out, down_out = add(up_out, up), add(down_out, down)
        up_out, down_out = after((up_out, down_out), *waits[step - 1])
        up = up_line(up_out, range(min(step, groups - 1)))
        down = down_line(down_out, range(max(groups - step, 1), groups))
    return add(terms[0].astype(jnp.float32) + up.astype(jnp.float32), down)


def per_device(tokens, cotangent, gate_weight, up_weight, down_weight):
    groups = lax.axis_size("local")
    nodes = lax.axis_size("node")
    me = lax.axis_index("local")
    node = lax.axis_index("node")
    rows, width = tokens.shape
    depth, unit_count = gate_weight.shape
    owned = unit_count // groups
    features = width // nodes
    grad_scale = 1.0 / math.sqrt(rows * groups)
    order = shift_order(groups)
    share = rows // nodes

    slices = jnp.stack(
        [lax.dynamic_slice_in_dim(a, node * share, share, 0) for a in (tokens, cotangent)]
    )
    def units(d):
        return d * owned

    def gate_piece(k):
        return lax.dynamic_slice(gate_weight, (0, units((me + k) % groups)), (depth, owned))

    def up_piece(k):
        return lax.dynamic_slice(up_weight, (0, units((me + k) % groups)), (depth, owned))

    def down_piece(k):
        return lax.dynamic_slice(down_weight, (units((me + k) % groups), 0), (owned, depth))

    gate_up = jnp.zeros((width, 2 * owned), jnp.bfloat16)
    down = jnp.zeros((owned, width), jnp.bfloat16)
    ready = {}
    for k in order:
        got = shift(gate_piece(k), k, groups)
        ready[k] = (got,)
        gate_up = lax.dynamic_update_slice(gate_up, got, (((me - k) % groups) * depth, 0))

    up_going = down_going = slices
    ups, downs = [], []
    for step in range(1, groups):
        if step == groups - 1:
            up_going, down_going = after((up_going, down_going), *ready[order[0]])
        up_going = up_line(up_going, range(step - 1, groups - 1))
        down_going = down_line(down_going, range(1, groups - step + 1))
        ups.append(up_going)
        downs.append(down_going)
    arrived = [jnp.where(me >= k, ups[k - 1], downs[groups - k - 1]) for k in range(1, groups)]
    tok_rest, cot_rest = (
        lax.all_gather(
            after(jnp.concatenate([a[i] for a in arrived], 0), *ready[order[1 + i]]),
            "node",
            axis=0,
            tiled=True,
        )
        for i in (0, 1)
    )
    for k in order:
        got = shift(after(up_piece(k), *ready[k]), k, groups)
        ready[k] = (got,)
        gate_up = lax.dynamic_update_slice(gate_up, got, (((me - k) % groups) * depth, owned))
    down_came = {}
    for k in order:
        down_came[k] = shift(after(down_piece(k), *ready[k]), k, groups)
        ready[k] = (down_came[k],)
    gate_up = lax.dynamic_update_slice(gate_up, gate_piece(0), (me * depth, 0))
    gate_up = lax.dynamic_update_slice(gate_up, up_piece(0), (me * depth, owned))

    toks, cots = (tokens, tok_rest), (cotangent, cot_rest)
    parts = [dot(t, gate_up, ((1,), (0,))) for t in toks]
    sigmas = [jax.nn.sigmoid(p[:, :owned]) for p in parts]
    actives = [p[:, :owned] * s for p, s in zip(parts, sigmas)]
    hiddens = [(a * p[:, owned:]).astype(jnp.bfloat16) for a, p in zip(actives, parts)]

    def summed(lefts, rights):
        return sum(dot(a, b, ((0,), (0,))) for a, b in zip(lefts, rights)) * grad_scale

    def columns(a, k):
        return lax.dynamic_slice_in_dim(a, ((me + k) % groups) * depth, depth, 1)

    down_grad = jnp.zeros((unit_count, depth), jnp.float32)
    down_terms = {
        k: summed(hiddens, [columns(c, k) for c in cots]).astype(jnp.bfloat16) for k in order
    }
    down = lax.dynamic_update_slice(down, down_piece(0), (0, me * depth))
    for k in order:
        came = after(down_came[k], *down_terms.values())
        down = lax.dynamic_update_slice(down, came, (0, ((me - k) % groups) * depth))
    for k in order:
        got = shift(after(down_terms[k], *ready[k]), k, groups)
        ready[k] = (got,)
        down_grad = lax.dynamic_update_slice(
            down_grad, got.astype(jnp.float32), (units((me - k) % groups), 0)
        )
    down_grad = lax.dynamic_update_slice(
        down_grad, summed(hiddens, [columns(c, 0) for c in cots]), (units(me), 0)
    )

    blocks = [k for k in range(groups) if k % 2] + [k for k in range(groups) if not k % 2]

    def by_block(own, rest):
        rest = rest.reshape(nodes, groups - 1, share, rest.shape[1])
        cut = {k + 1: rest[:, k].reshape(own.shape) for k in range(groups - 1)}
        cut[0] = own
        return jnp.concatenate([cut[k] for k in blocks], 0)

    def near(a, axis, other):
        return jnp.concatenate(
            [
                lax.dynamic_slice_in_dim(a, (node ^ (r + other)) * features, features, axis)
                for r in NEAR
            ],
            axis,
        )

    def out_term(weights):
        return dot(hidden_rows, weights, ((1,), (0,))).astype(jnp.bfloat16)

    def in_term(weights):
        return dot(both_rows, weights, ((1,), (1,))).astype(jnp.bfloat16)

    near_known = nodes == 8
    hidden_rows = by_block(*hiddens)
    if near_known:
        out_first = out_sent = out_term(near(down, 1, 1))
        out_kept = out_term(near(down, 1, 0))
    else:
        out_first = out_term(down)

    down_then = after(down, out_first)
    backs = [dot(c, down_then, ((1,), (1,))) for c in cots]
    gate_backs = [
        (b * p[:, owned:] * s * (1.0 + p[:, :owned] * (1.0 - s))).astype(jnp.bfloat16)
        for b, p, s in zip(backs, parts, sigmas)
    ]
    up_backs = [(b * a).astype(jnp.bfloat16) for b, a in zip(backs, actives)]
    both = [jnp.concatenate(g, 1) for g in zip(gate_backs, up_backs)]

    gate_up_terms = {
        order[0]: summed([columns(t, order[0]) for t in toks], both).astype(jnp.bfloat16)
    }
    both_rows = after(by_block(*both), gate_up_terms[order[0]])
    if near_known:
        in_first = in_sent = in_term(near(gate_up, 0, 1))
        in_kept = in_term(near(gate_up, 0, 0))
    else:
        in_first = in_term(gate_up)
    both = after(tuple(both), in_first)
    for k in order[1:]:
        gate_up_terms[k] = summed([columns(t, k) for t in toks], both).astype(jnp.bfloat16)

    passed = [ready[k][0] for k in order]
    if near_known:
        out_sums, came = node_sum(out_sent, out_kept, nodes, passed)
        in_sums, _ = node_sum(in_sent, in_kept, nodes, came)
    else:
        out_sums, in_sums = (
            jnp.split(
                lax.psum_scatter(t, "node", scatter_dimension=1, tiled=True), 2, 0
            )
            for t in (out_first, in_first)
        )

    gate_grad = jnp.zeros((depth, unit_count), jnp.float32)
    up_grad = jnp.zeros((depth, unit_count), jnp.float32)
    for k in order:
        ready[k] = (shift(after(gate_up_terms[k], *ready[k]), k, groups),)
        got = ready[k][0].astype(jnp.float32)
        at = (0, units((me - k) % groups))
        gate_grad = lax.dynamic_update_slice(gate_grad, got[:, :owned], at)
        up_grad = lax.dynamic_update_slice(up_grad, got[:, owned:], at)
    term = summed([columns(t, 0) for t in toks], both)
    gate_grad = lax.dynamic_update_slice(gate_grad, term[:, :owned], (0, units(me)))
    up_grad = lax.dynamic_update_slice(up_grad, term[:, owned:], (0, units(me)))

    def finish(halves, waits):
        terms = {}
        for i, k in enumerate(blocks):
            at = i % (groups // 2)
            terms[k] = halves[2 * i // groups][at * rows : (at + 1) * rows]
        return line_sum(terms, groups, waits)

    block_out = finish(out_sums, [()] * groups)
    input_grad = finish(in_sums, [ready[k] for k in order])
    return (block_out, input_grad, gate_grad, up_grad, down_grad)


def solution(mesh):
    placed = (
        P("local", None),
        P("local", None),
        P("local", "node"),
        P("local", "node"),
        P("node", "local"),
    )
    return jax.shard_map(
        per_device,
        mesh=mesh,
        in_specs=placed,
        out_specs=(
            P("local", "node"),
            P("local", "node"),
            P("local", "node"),
            P("local", "node"),
            P("node", "local"),
        ),
        check_vma=False,
    )
```

time: 1490 us -> 746 us (0.50)
  waiting for transfers between devices: 1290 us -> 382 us
  starting transfers between devices: 0.24 us -> 103 us
  local copies, waits for them, and re-layouts: 29.5 us -> 59.1 us
  matrix products: 113 us -> 133 us
    reduce_scatter x3 -> x0, waiting for transfers between devices: 651 us -> none  [the longest x1 581 us: per_device(): lax.psum_scatter((jnp.concatenate((first, second), 1) * grad_scale).astyp...]
    all_gather x3 -> x2, waiting for transfers between devices: 633 us -> 7.43 us  [per_device(): lax.all_gather(after(jnp.concatenate([a[i] for a in arrived], 0), *ready[...]
    ppermute x0 -> x43, waiting for transfers between devices: none -> 375 us  [the longest x15 270 us: shift(): lax.ppermute(value, 'local', [(i, (i + step) % groups) for i in range(gro...]
    ppermute x0 -> x43, starting transfers between devices: none -> 103 us  [the longest x15 50.5 us: shift(): lax.ppermute(value, 'local', [(i, (i + step) % groups) for i in range(gro...]
    dot_general x8 -> x24, matrix products: 113 us -> 133 us  [dot(): lax.dot_general(left, right, (dims, ((), ())), preferred_element_type=jnp...]
    convert_element_type x2 -> x19, other arithmetic: 50.1 us -> 33.3 us  [the longest x14 29.3 us: add(): return (a.astype(jnp.float32) + b.astype(jnp.float32)).astype(jnp.bfloat16)]
  transfers between devices with their start and end apart: 6 -> 45, of which waited for: 6 -> 21; matrix products, arithmetic and copies ran while one was open for 7% -> 28% of each run, Pallas kernels for 0% -> 0%
where the time goes in v2:
time: 746 us; the launch traced here: 740 us
  waiting for transfers between devices  382 us (51%)
  matrix products  133 us (18%)
  starting transfers between devices  103 us (14%)
  local copies, waits for them, and re-layouts  59.1 us (8%)
  other arithmetic  47.9 us (6%)
  between operations  15.4 us (2%)
    ppermute x15, waiting for transfers between devices, shift(): lax.ppermute(value, 'local', [(i, (i + step) % groups) for i in range(gro...  270 us
    dot_general x24, matrix products, dot(): lax.dot_general(left, right, (dims, ((), ())), preferred_element_type=jnp...  133 us
    ppermute x15, starting transfers between devices, shift(): lax.ppermute(value, 'local', [(i, (i + step) % groups) for i in range(gro...  50.5 us
    ppermute x9, waiting for transfers between devices, up_line(): return lax.ppermute(value, 'local', [(i, i + 1) for i in senders])  45 us
    ppermute x10, waiting for transfers between devices, swap(): return lax.ppermute(value, 'node', [(i, i ^ bit) for i in range(nodes)])  37.1 us
    ppermute x9, starting transfers between devices, up_line(): return lax.ppermute(value, 'local', [(i, i + 1) for i in senders])  32.6 us
    convert_element_type x14, other arithmetic, add(): return (a.astype(jnp.float32) + b.astype(jnp.float32)).astype(jnp.bfloat16)  29.3 us
    ppermute x9, waiting for transfers between devices, down_line(): return lax.ppermute(value, 'local', [(i, i - 1) for i in senders])  22.9 us
  transfers between devices with their start and end apart: 45, of which 21 were waited for; matrix products, arithmetic and copies ran while one was open for 28% of the time, Pallas kernels for 0%

profile of v2, /device:TPU:0, one launch (start us, length us, event | category | flops | bytes accessed | tf_op | source)
XLA Modules:
  0.0 740.5 jit_solution(1230158297424204517)
XLA Ops:
  8.8 5.9 collective-permute-start
  16.0 20.1 %collective-permute-done = bf16[2,64,4096]{2,1,0:T(8,128)(2,1)} collective-permute-done((bf16[2,64,4096]{2,1,0:T(8,128)(2,1)S(1)}, bf16[2,64,4096]{2,1,0:T(8,128)(2,1)}, u32[]{:S(2)}, u32[]{:S(2)}) %collective-permute-start) | collective-permute-done | bytes 1048608 | tf_op jit(solution)/shard_map/ppermute | solution.py:22
  44.1 4.8 collective-permute-start.4
  49.0 70.0 %collective-permute-done.4 = bf16[1024,384]{1,0:T(8,128)(2,1)S(1)} collective-permute-done((bf16[1024,384]{1,0:T(8,128)(2,1)}, bf16[1024,384]{1,0:T(8,128)(2,1)S(1)}, u32[]{:S(2)}, u32[]{:S(2)}) %collective-permute-start.4) | collective-permute-done | bytes 786464 | tf_op jit(solution)/shard_map/ppermute | solution.py:18
  125.5 19.2 %collective-permute-done.5 = bf16[2,64,4096]{2,1,0:T(8,128)(2,1)S(1)} collective-permute-done((bf16[2,64,4096]{2,1,0:T(8,128)(2,1)}, bf16[2,64,4096]{2,1,0:T(8,128)(2,1)S(1)}, u32[]{:S(2)}, u32[]{:S(2)}) %collective-permute-start.5) | collective-permute-done | bytes 1048608 | tf_op jit(solution)/shard_map/ppermute | solution.py:26
  150.2 13.5 %collective-permute-done.8 = bf16[1024,384]{1,0:T(8,128)(2,1)} collective-permute-done((bf16[1024,384]{1,0:T(8,128)(2,1)}, bf16[1024,384]{1,0:T(8,128)(2,1)}, u32[]{:S(2)}, u32[]{:S(2)}) %collective-permute-start.8) | collective-permute-done | bytes 786464 | tf_op jit(solution)/shard_map/ppermute | solution.py:18
  176.7 64.6 %collective-permute-done.9 = bf16[1024,384]{1,0:T(8,128)(2,1)} collective-permute-done((bf16[1024,384]{1,0:T(8,128)(2,1)}, bf16[1024,384]{1,0:T(8,128)(2,1)}, u32[]{:S(2)}, u32[]{:S(2)}) %collective-permute-start.9) | collective-permute-done | bytes 786464 | tf_op jit(solution)/shard_map/ppermute | solution.py:18
  266.7 14.4 %fusion.106 = f32[1536,768]{1,0:T(8,128)S(1)} fusion(bf16[1536,4096]{1,0:T(8,128)(2,1)} %all-gather.3.cloned.1.call-done, bf16[4096,768]{1,0:T(8,128)(2,1)} %copy-done), kind=kOutput, calls=%fused_computation.212 | convolution fusion | flops 9663676416 | bytes 23592960 | tf_op jit(solution)/shard_map/dot_general | solution.py:10
  285.0 7.4 %all-gather.5.cloned.1.call-done = bf16[1536,4096]{1,0:T(8,128)(2,1)} async-done(((bf16[192,4096]{1,0:T(8,128)(2,1)}), bf16[1536,4096]{1,0:T(8,128)(2,1)}) %all-gather.5.cloned.1.call-update) | async-done | bytes 12582928 | tf_op jit(solution)/shard_map/all_gather | solution.py:120
  292.4 5.2 multiply_convert_fusion.8
  318.4 9.8 %convolution_convert_fusion.2 = bf16[2048,2048]{1,0:T(8,128)(2,1)} fusion(bf16[384,512]{1,0:T(8,128)(2,1)} %get-tuple-element.108, bf16[384,512]{1,0:T(8,128)(2,1)} %get-tuple-element.109, bf16[384,512]{1,0:T(8,128)(2,1)} %get-tuple-element.110, bf16[384,512]{1,0:T(8,128)(2,1)} %get-tuple-element.111, bf16[512,384]{0,1:T(8,128)(2,1)} %copy.23, ...), kind=kOutput, calls=%fused_computation.2 | convolution fusion | flops 3238002688 | bytes 11534336 | tf_op jit(solution)/shard_map/dot_general | solution.py:10
  331.4 11.3 %multiply_convert_fusion.4 = (bf16[1536,384]{1,0:T(8,128)(2,1)S(1)}, bf16[1536,384]{1,0:T(8,128)(2,1)S(1)}) fusion(f32[1536,768]{1,0:T(8,128)} %copy-done.6, bf16[1536,4096]{1,0:T(8,128)(2,1)} %all-gather.5.cloned.1.call-done, bf16[384,4096]{1,0:T(8,128)(2,1)S(1)} %constant_dynamic-update-slice_fusion), kind=kOutput, calls=%fused_computation.45 | convolution fusion | flops 4839505920 | bytes 22806528 | tf_op jit(solution)/shard_map/dot_general | solution.py:10
  357.6 6.0 multiply_convert_fusion.2
  363.7 11.6 %convolution_convert_fusion = bf16[2048,2048]{1,0:T(8,128)(2,1)} fusion(bf16[2048,768]{0,1:T(8,128)(2,1)S(1)} %pad_maximum_fusion, bf16[512,768]{1,0:T(8,128)(2,1)S(1)} %copy-done.32, bf16[512,768]{1,0:T(8,128)(2,1)S(1)} %copy-done.33, bf16[512,768]{1,0:T(8,128)(2,1)S(1)} %copy-done.34, bf16[512,768]{1,0:T(8,128)(2,1)S(1)} %copy-done.35), kind=kOutput, calls=%fused_computation | convolution fusion | flops 6459228160 | bytes 14680064 | tf_op jit(solution)/shard_map/dot_general | solution.py:10
  378.6 16.1 %collective-permute-start.16 = (bf16[384,1024]{1,0:T(8,128)(2,1)}, bf16[384,1024]{1,0:T(8,128)(2,1)S(1)}, u32[]{:S(2)}, u32[]{:S(2)}) collective-permute-start(bf16[384,1024]{1,0:T(8,128)(2,1)} %multiply_convert_fusion.8), channel_id=1, source_target_pairs={{0,2},{1,3},{2,0},{3,1},{4,6},{5,7},{6,4},{7,5},{8,10},{9,11},{10,... | collective-permute-start | bytes 2359304 | tf_op jit(solution)/shard_map/ppermute | solution.py:18
  401.3 5.4 convolution_convert_fusion.3
  406.6 5.8 multiply_convert_fusion.1
  412.5 4.8 add_convert_fusion.2
  417.3 29.7 %collective-permute-done.16 = bf16[384,1024]{1,0:T(8,128)(2,1)S(1)} collective-permute-done((bf16[384,1024]{1,0:T(8,128)(2,1)}, bf16[384,1024]{1,0:T(8,128)(2,1)S(1)}, u32[]{:S(2)}, u32[]{:S(2)}) %collective-permute-start.16) | collective-permute-done | bytes 786464 | tf_op jit(solution)/shard_map/ppermute | solution.py:18
  454.7 11.3 %convolution_convert_fusion.1 = bf16[2048,2048]{1,0:T(8,128)(2,1)S(1)} fusion(bf16[2048,768]{0,1:T(8,128)(2,1)} %copy-done.10, bf16[512,768]{1,0:T(8,128)(2,1)S(1)} %copy-done.29, bf16[512,768]{1,0:T(8,128)(2,1)S(1)} %copy-done.30, bf16[512,768]{1,0:T(8,128)(2,1)S(1)} %copy-done.31, bf16[512,768]{1,0:T(8,128)(2,1)S(1)} %copy-done.28), kind=kOutput, calls=%fused_computation.1 | convolution fusion | flops 6459228160 | bytes 14680064 | tf_op jit(solution)/shard_map/dot_general | solution.py:10
  470.2 23.9 %collective-permute-done.19 = bf16[1024,1024]{1,0:T(8,128)(2,1)} collective-permute-done((bf16[1024,1024]{1,0:T(8,128)(2,1)}, bf16[1024,1024]{1,0:T(8,128)(2,1)}, u32[]{:S(2)}, u32[]{:S(2)}) %collective-permute-start.19) | collective-permute-done | bytes 2097184 | tf_op jit(solution)/shard_map/ppermute | solution.py:38
  495.9 5.8 multiply_convert_fusion
  504.2 17.1 %collective-permute-start.34 = (bf16[1024,768]{1,0:T(8,128)(2,1)S(1)}, bf16[1024,768]{1,0:T(8,128)(2,1)S(1)}, u32[]{:S(2)}, u32[]{:S(2)}) collective-permute-start(bf16[1024,768]{1,0:T(8,128)(2,1)S(1)} %copy-done.54), channel_id=1, source_target_pairs={{0,2},{1,3},{2,0},{3,1},{4,6},{5,7},{6,4},{7,5},{8,10},{9,11},{10,... | collective-permute-start | bytes 4718600 | tf_op jit(solution)/shard_map/ppermute | solution.py:18
  521.2 6.3 add_multiply_fusion
  545.3 77.7 %collective-permute-done.34 = bf16[1024,768]{1,0:T(8,128)(2,1)S(1)} collective-permute-done((bf16[1024,768]{1,0:T(8,128)(2,1)S(1)}, bf16[1024,768]{1,0:T(8,128)(2,1)S(1)}, u32[]{:S(2)}, u32[]{:S(2)}) %collective-permute-start.34) | collective-permute-done | bytes 1572896 | tf_op jit(solution)/shard_map/ppermute | solution.py:18
  641.7 14.2 %collective-permute-done.40 = bf16[1024,768]{1,0:T(8,128)(2,1)} collective-permute-done((bf16[1024,768]{1,0:T(8,128)(2,1)}, bf16[1024,768]{1,0:T(8,128)(2,1)}, u32[]{:S(2)}, u32[]{:S(2)}) %collective-permute-start.40) | collective-permute-done | bytes 1572896 | tf_op jit(solution)/shard_map/ppermute | solution.py:18
  665.9 9.4 %collective-permute-done.33 = bf16[1024,512]{1,0:T(8,128)(2,1)} collective-permute-done((bf16[1024,512]{1,0:T(8,128)(2,1)S(1)}, bf16[1024,512]{1,0:T(8,128)(2,1)}, u32[]{:S(2)}, u32[]{:S(2)}) %collective-permute-start.33) | collective-permute-done | bytes 1048608 | tf_op jit(solution)/shard_map/ppermute | solution.py:38
  685.5 9.0 %collective-permute-done.35 = bf16[512,512]{1,0:T(8,128)(2,1)S(1)} collective-permute-done((bf16[512,512]{1,0:T(8,128)(2,1)S(1)}, bf16[512,512]{1,0:T(8,128)(2,1)S(1)}, u32[]{:S(2)}, u32[]{:S(2)}) %collective-permute-start.35) | collective-permute-done | bytes 524320 | tf_op jit(solution)/shard_map/ppermute | solution.py:22
  695.4 5.0 collective-permute-start.38
  700.9 4.8 collective-permute-done.25
  707.2 5.0 collective-permute-start.27
  718.5 5.0 collective-permute-start.41
  (272 shorter events, 204.8 us)
Async XLA Ops:
  7.2 259.5 %all-gather.3.cloned.1.call-start = ((), (), s32[]{:S(2)}) async-start(), calls=%async_computation | async-start | bytes 14155776 | tf_op jit(solution)/shard_map/all_gather | solution.py:120
  8.8 27.3 %collective-permute-start = (bf16[2,64,4096]{2,1,0:T(8,128)(2,1)S(1)}, bf16[2,64,4096]{2,1,0:T(8,128)(2,1)}, u32[]{:S(2)}, u32[]{:S(2)}) collective-permute-start(bf16[2,64,4096]{2,1,0:T(8,128)(2,1)S(1)} %pad_maximum_fusion.5), channel_id=1, source_target_pairs={{0,1},{1,2},{2,3},{4,5},{5,6},{6,7},{8,9},{9,10},{10,11},{12,13},{... | collective-permute-start | bytes 3145736 | tf_op jit(solution)/shard_map/ppermute | solution.py:22
  14.7 26.6 %collective-permute-start.2 = (bf16[2,64,4096]{2,1,0:T(8,128)(2,1)S(1)}, bf16[2,64,4096]{2,1,0:T(8,128)(2,1)}, u32[]{:S(2)}, u32[]{:S(2)}) collective-permute-start(bf16[2,64,4096]{2,1,0:T(8,128)(2,1)S(1)} %pad_maximum_fusion.5), channel_id=1, source_target_pairs={{1,0},{2,1},{3,2},{5,4},{6,5},{7,6},{9,8},{10,9},{11,10},{13,12},{... | collective-permute-start | bytes 3145736 | tf_op jit(solution)/shard_map/ppermute | solution.py:26
  36.1 82.9 %collective-permute-start.1 = (bf16[2,64,4096]{2,1,0:T(8,128)(2,1)}, bf16[2,64,4096]{2,1,0:T(8,128)(2,1)}, u32[]{:S(2)}, u32[]{:S(2)}) collective-permute-start(bf16[2,64,4096]{2,1,0:T(8,128)(2,1)} %collective-permute-done), channel_id=1, source_target_pairs={{1,2},{2,3},{5,6},{6,7},{9,10},{10,11},{13,14},{14,15},{17,18},{18... | collective-permute-start | bytes 3145736 | tf_op jit(solution)/shard_map/ppermute | solution.py:22
  41.3 77.7 %collective-permute-start.3 = (bf16[2,64,4096]{2,1,0:T(8,128)(2,1)}, bf16[2,64,4096]{2,1,0:T(8,128)(2,1)}, u32[]{:S(2)}, u32[]{:S(2)}) collective-permute-start(bf16[2,64,4096]{2,1,0:T(8,128)(2,1)} %collective-permute-done.2), channel_id=1, source_target_pairs={{1,0},{2,1},{5,4},{6,5},{9,8},{10,9},{13,12},{14,13},{17,16},{18,1... | collective-permute-start | bytes 3145736 | tf_op jit(solution)/shard_map/ppermute | solution.py:26
  44.1 74.9 %collective-permute-start.4 = (bf16[1024,384]{1,0:T(8,128)(2,1)}, bf16[1024,384]{1,0:T(8,128)(2,1)S(1)}, u32[]{:S(2)}, u32[]{:S(2)}) collective-permute-start(bf16[1024,384]{1,0:T(8,128)(2,1)} %get-tuple-element.124), channel_id=1, source_target_pairs={{0,2},{1,3},{2,0},{3,1},{4,6},{5,7},{6,4},{7,5},{8,10},{9,11},{10,... | collective-permute-start | bytes 2359304 | tf_op jit(solution)/shard_map/ppermute | solution.py:18
  49.0 98.0 %collective-permute-start.7 = (bf16[1024,384]{1,0:T(8,128)(2,1)}, bf16[1024,384]{1,0:T(8,128)(2,1)}, u32[]{:S(2)}, u32[]{:S(2)}) collective-permute-start(bf16[1024,384]{1,0:T(8,128)(2,1)} %get-tuple-element.123), channel_id=1, source_target_pairs={{0,1},{1,2},{2,3},{3,0},{4,5},{5,6},{6,7},{7,4},{8,9},{9,10},{10,1... | collective-permute-start | bytes 2359304 | tf_op jit(solution)/shard_map/ppermute | solution.py:18
  119.8 24.9 %collective-permute-start.5 = (bf16[2,64,4096]{2,1,0:T(8,128)(2,1)}, bf16[2,64,4096]{2,1,0:T(8,128)(2,1)S(1)}, u32[]{:S(2)}, u32[]{:S(2)}) collective-permute-start(bf16[2,64,4096]{2,1,0:T(8,128)(2,1)} %collective-permute-done.3), channel_id=1, source_target_pairs={{1,0},{5,4},{9,8},{13,12},{17,16},{21,20},{25,24},{29,28}} | collective-permute-start | bytes 3145736 | tf_op jit(solution)/shard_map/ppermute | solution.py:26
  147.0 145.4 %all-gather.5.cloned.1.call-start = ((), (), s32[]{:S(2)}) async-start(), calls=%async_computation.1 | async-start | bytes 14155776 | tf_op jit(solution)/shard_map/all_gather | solution.py:120
  165.2 76.1 %collective-permute-start.9 = (bf16[1024,384]{1,0:T(8,128)(2,1)}, bf16[1024,384]{1,0:T(8,128)(2,1)}, u32[]{:S(2)}, u32[]{:S(2)}) collective-permute-start(bf16[1024,384]{1,0:T(8,128)(2,1)} %get-tuple-element.47), channel_id=1, source_target_pairs={{0,2},{1,3},{2,0},{3,1},{4,6},{5,7},{6,4},{7,5},{8,10},{9,11},{10,... | collective-permute-start | bytes 2359304 | tf_op jit(solution)/shard_map/ppermute | solution.py:18
  165.2 76.1 %collective-permute-start.10 = (bf16[1024,384]{1,0:T(8,128)(2,1)}, bf16[1024,384]{1,0:T(8,128)(2,1)}, u32[]{:S(2)}, u32[]{:S(2)}) collective-permute-start(bf16[1024,384]{1,0:T(8,128)(2,1)} %get-tuple-element.48), channel_id=1, source_target_pairs={{0,1},{1,2},{2,3},{3,0},{4,5},{5,6},{6,7},{7,4},{8,9},{9,10},{10,1... | collective-permute-start | bytes 2359304 | tf_op jit(solution)/shard_map/ppermute | solution.py:18
  168.1 73.2 %collective-permute-start.11 = (bf16[1024,384]{1,0:T(8,128)(2,1)}, bf16[1024,384]{1,0:T(8,128)(2,1)}, u32[]{:S(2)}, u32[]{:S(2)}) collective-permute-start(bf16[1024,384]{1,0:T(8,128)(2,1)} %get-tuple-element.49), channel_id=1, source_target_pairs={{0,3},{1,0},{2,1},{3,2},{4,7},{5,4},{6,5},{7,6},{8,11},{9,8},{10,9... | collective-permute-start | bytes 2359304 | tf_op jit(solution)/shard_map/ppermute | solution.py:18
  241.3 64.9 %collective-permute-start.12 = (bf16[384,1024]{1,0:T(8,128)(2,1)}, bf16[384,1024]{1,0:T(8,128)(2,1)}, u32[]{:S(2)}, u32[]{:S(2)}) collective-permute-start(bf16[384,1024]{1,0:T(8,128)(2,1)} %get-tuple-element.50), channel_id=1, source_target_pairs={{0,2},{1,3},{2,0},{3,1},{4,6},{5,7},{6,4},{7,5},{8,10},{9,11},{10,... | collective-permute-start | bytes 2359304 | tf_op jit(solution)/shard_map/ppermute | solution.py:18
  241.3 64.9 %collective-permute-start.13 = (bf16[384,1024]{1,0:T(8,128)(2,1)}, bf16[384,1024]{1,0:T(8,128)(2,1)}, u32[]{:S(2)}, u32[]{:S(2)}) collective-permute-start(bf16[384,1024]{1,0:T(8,128)(2,1)} %get-tuple-element.53), channel_id=1, source_target_pairs={{0,1},{1,2},{2,3},{3,0},{4,5},{5,6},{6,7},{7,4},{8,9},{9,10},{10,1... | collective-permute-start | bytes 2359304 | tf_op jit(solution)/shard_map/ppermute | solution.py:18
  241.3 64.9 %collective-permute-start.14 = (bf16[384,1024]{1,0:T(8,128)(2,1)}, bf16[384,1024]{1,0:T(8,128)(2,1)}, u32[]{:S(2)}, u32[]{:S(2)}) collective-permute-start(bf16[384,1024]{1,0:T(8,128)(2,1)} %get-tuple-element.55), channel_id=1, source_target_pairs={{0,3},{1,0},{2,1},{3,2},{4,7},{5,4},{6,5},{7,6},{8,11},{9,8},{10,9... | collective-permute-start | bytes 2359304 | tf_op jit(solution)/shard_map/ppermute | solution.py:18
  328.2 84.3 %collective-permute-start.15 = (bf16[2048,2048]{1,0:T(8,128)(2,1)}, bf16[2048,2048]{1,0:T(8,128)(2,1)}, u32[]{:S(2)}, u32[]{:S(2)}) collective-permute-start(bf16[2048,2048]{1,0:T(8,128)(2,1)} %convolution_convert_fusion.2), channel_id=1, source_target_pairs={{0,4},{4,0},{8,12},{12,8},{16,20},{20,16},{24,28},{28,24},{1,5},{5... | collective-permute-start | bytes 25165832 | tf_op jit(solution)/shard_map/ppermute | solution.py:38
  375.3 90.8 %collective-permute-start.29 = (bf16[2048,2048]{1,0:T(8,128)(2,1)}, bf16[2048,2048]{1,0:T(8,128)(2,1)}, u32[]{:S(2)}, u32[]{:S(2)}) collective-permute-start(bf16[2048,2048]{1,0:T(8,128)(2,1)} %convolution_convert_fusion), channel_id=1, source_target_pairs={{0,4},{4,0},{8,12},{12,8},{16,20},{20,16},{24,28},{28,24},{1,5},{5... | collective-permute-start | bytes 25165832 | tf_op jit(solution)/shard_map/ppermute | solution.py:38
  378.6 68.4 %collective-permute-start.16 = (bf16[384,1024]{1,0:T(8,128)(2,1)}, bf16[384,1024]{1,0:T(8,128)(2,1)S(1)}, u32[]{:S(2)}, u32[]{:S(2)}) collective-permute-start(bf16[384,1024]{1,0:T(8,128)(2,1)} %multiply_convert_fusion.8), channel_id=1, source_target_pairs={{0,2},{1,3},{2,0},{3,1},{4,6},{5,7},{6,4},{7,5},{8,10},{9,11},{10,... | collective-permute-start | bytes 2359304 | tf_op jit(solution)/shard_map/ppermute | solution.py:18
  394.6 52.3 %collective-permute-start.17 = (bf16[384,1024]{1,0:T(8,128)(2,1)}, bf16[384,1024]{1,0:T(8,128)(2,1)S(1)}, u32[]{:S(2)}, u32[]{:S(2)}) collective-permute-start(bf16[384,1024]{1,0:T(8,128)(2,1)} %multiply_convert_fusion.7), channel_id=1, source_target_pairs={{0,1},{1,2},{2,3},{3,0},{4,5},{5,6},{6,7},{7,4},{8,9},{9,10},{10,1... | collective-permute-start | bytes 2359304 | tf_op jit(solution)/shard_map/ppermute | solution.py:18
  394.6 52.4 %collective-permute-start.18 = (bf16[384,1024]{1,0:T(8,128)(2,1)}, bf16[384,1024]{1,0:T(8,128)(2,1)S(1)}, u32[]{:S(2)}, u32[]{:S(2)}) collective-permute-start(bf16[384,1024]{1,0:T(8,128)(2,1)} %multiply_convert_fusion.6), channel_id=1, source_target_pairs={{0,3},{1,0},{2,1},{3,2},{4,7},{5,4},{6,5},{7,6},{8,11},{9,8},{10,9... | collective-permute-start | bytes 2359304 | tf_op jit(solution)/shard_map/ppermute | solution.py:18
  447.1 47.0 %collective-permute-start.19 = (bf16[1024,1024]{1,0:T(8,128)(2,1)}, bf16[1024,1024]{1,0:T(8,128)(2,1)}, u32[]{:S(2)}, u32[]{:S(2)}) collective-permute-start(bf16[1024,1024]{1,0:T(8,128)(2,1)} %get-tuple-element.60), channel_id=1, source_target_pairs={{0,16},{4,20},{8,24},{12,28},{16,0},{20,4},{24,8},{28,12},{1,17},{... | collective-permute-start | bytes 6291464 | tf_op jit(solution)/shard_map/ppermute | solution.py:38
  449.2 46.4 %collective-permute-start.21 = (bf16[1024,1024]{1,0:T(8,128)(2,1)}, bf16[1024,1024]{1,0:T(8,128)(2,1)}, u32[]{:S(2)}, u32[]{:S(2)}) collective-permute-start(bf16[1024,1024]{1,0:T(8,128)(2,1)} %get-tuple-element.61), channel_id=1, source_target_pairs={{0,8},{4,12},{8,0},{12,4},{16,24},{20,28},{24,16},{28,20},{1,9},{5... | collective-permute-start | bytes 6291464 | tf_op jit(solution)/shard_map/ppermute | solution.py:38
  495.6 45.1 %collective-permute-start.30 = (bf16[1024,1024]{1,0:T(8,128)(2,1)S(1)}, bf16[1024,1024]{1,0:T(8,128)(2,1)S(1)}, u32[]{:S(2)}, u32[]{:S(2)}) collective-permute-start(bf16[1024,1024]{1,0:T(8,128)(2,1)S(1)} %get-tuple-element.70), channel_id=1, source_target_pairs={{0,16},{4,20},{8,24},{12,28},{16,0},{20,4},{24,8},{28,12},{1,17},{... | collective-permute-start | bytes 6291464 | tf_op jit(solution)/shard_map/ppermute | solution.py:38
  504.2 118.8 %collective-permute-start.34 = (bf16[1024,768]{1,0:T(8,128)(2,1)S(1)}, bf16[1024,768]{1,0:T(8,128)(2,1)S(1)}, u32[]{:S(2)}, u32[]{:S(2)}) collective-permute-start(bf16[1024,768]{1,0:T(8,128)(2,1)S(1)} %copy-done.54), channel_id=1, source_target_pairs={{0,2},{1,3},{2,0},{3,1},{4,6},{5,7},{6,4},{7,5},{8,10},{9,11},{10,... | collective-permute-start | bytes 4718600 | tf_op jit(solution)/shard_map/ppermute | solution.py:18
  527.6 113.9 %collective-permute-start.37 = (bf16[1024,768]{1,0:T(8,128)(2,1)}, bf16[1024,768]{1,0:T(8,128)(2,1)S(1)}, u32[]{:S(2)}, u32[]{:S(2)}) collective-permute-start(bf16[1024,768]{1,0:T(8,128)(2,1)} %multiply_convert_fusion.1), channel_id=1, source_target_pairs={{0,1},{1,2},{2,3},{3,0},{4,5},{5,6},{6,7},{7,4},{8,9},{9,10},{10,1... | collective-permute-start | bytes 4718600 | tf_op jit(solution)/shard_map/ppermute | solution.py:18
  528.0 105.7 %collective-permute-start.32 = (bf16[1024,1024]{1,0:T(8,128)(2,1)S(1)}, bf16[1024,1024]{1,0:T(8,128)(2,1)S(1)}, u32[]{:S(2)}, u32[]{:S(2)}) collective-permute-start(bf16[1024,1024]{1,0:T(8,128)(2,1)S(1)} %get-tuple-element.71), channel_id=1, source_target_pairs={{0,8},{4,12},{8,0},{12,4},{16,24},{20,28},{24,16},{28,20},{1,9},{5... | collective-permute-start | bytes 6291464 | tf_op jit(solution)/shard_map/ppermute | solution.py:38
  536.5 91.4 %collective-permute-start.20 = (bf16[1024,512]{1,0:T(8,128)(2,1)S(1)}, bf16[1024,512]{1,0:T(8,128)(2,1)S(1)}, u32[]{:S(2)}, u32[]{:S(2)}) collective-permute-start(bf16[1024,512]{1,0:T(8,128)(2,1)S(1)} %add_convert_fusion.20), channel_id=1, source_target_pairs={{0,8},{4,12},{8,0},{12,4},{16,24},{20,28},{24,16},{28,20},{1,9},{5... | collective-permute-start | bytes 3145736 | tf_op jit(solution)/shard_map/ppermute | solution.py:38
  542.4 91.3 %collective-permute-start.31 = (bf16[1024,512]{1,0:T(8,128)(2,1)S(1)}, bf16[1024,512]{1,0:T(8,128)(2,1)S(1)}, u32[]{:S(2)}, u32[]{:S(2)}) collective-permute-start(bf16[1024,512]{1,0:T(8,128)(2,1)S(1)} %add_convert_fusion.10), channel_id=1, source_target_pairs={{0,8},{4,12},{8,0},{12,4},{16,24},{20,28},{24,16},{28,20},{1,9},{5... | collective-permute-start | bytes 3145736 | tf_op jit(solution)/shard_map/ppermute | solution.py:38
  623.0 33.0 %collective-permute-start.40 = (bf16[1024,768]{1,0:T(8,128)(2,1)}, bf16[1024,768]{1,0:T(8,128)(2,1)}, u32[]{:S(2)}, u32[]{:S(2)}) collective-permute-start(bf16[1024,768]{1,0:T(8,128)(2,1)} %multiply_convert_fusion), channel_id=1, source_target_pairs={{0,3},{1,0},{2,1},{3,2},{4,7},{5,4},{6,5},{7,6},{8,11},{9,8},{10,9... | collective-permute-start | bytes 4718600 | tf_op jit(solution)/shard_map/ppermute | solution.py:18
  632.1 26.5 %collective-permute-start.22 = (bf16[1024,512]{1,0:T(8,128)(2,1)}, bf16[1024,512]{1,0:T(8,128)(2,1)}, u32[]{:S(2)}, u32[]{:S(2)}) collective-permute-start(bf16[1024,512]{1,0:T(8,128)(2,1)} %get-tuple-element.88), channel_id=1, source_target_pairs={{0,16},{4,20},{8,24},{12,28},{16,0},{20,4},{24,8},{28,12},{1,17},{... | collective-permute-start | bytes 3145736 | tf_op jit(solution)/shard_map/ppermute | solution.py:38
  637.3 38.0 %collective-permute-start.33 = (bf16[1024,512]{1,0:T(8,128)(2,1)S(1)}, bf16[1024,512]{1,0:T(8,128)(2,1)}, u32[]{:S(2)}, u32[]{:S(2)}) collective-permute-start(bf16[1024,512]{1,0:T(8,128)(2,1)S(1)} %get-tuple-element.84), channel_id=1, source_target_pairs={{0,16},{4,20},{8,24},{12,28},{16,0},{20,4},{24,8},{28,12},{1,17},{... | collective-permute-start | bytes 3145736 | tf_op jit(solution)/shard_map/ppermute | solution.py:38
  683.5 22.1 %collective-permute-start.25 = (bf16[512,512]{1,0:T(8,128)(2,1)S(1)}, bf16[512,512]{1,0:T(8,128)(2,1)S(1)}, u32[]{:S(2)}, u32[]{:S(2)}) collective-permute-start(bf16[512,512]{1,0:T(8,128)(2,1)S(1)} %get-tuple-element.64), channel_id=1, source_target_pairs={{0,1},{1,2},{4,5},{5,6},{8,9},{9,10},{12,13},{13,14},{16,17},{17,1... | collective-permute-start | bytes 1572872 | tf_op jit(solution)/shard_map/ppermute | solution.py:22
  (71 other events, 874.1 us)
Sparse Core Ops, SparseCore 0:
  147.1 70.6 all-gather.2
  220.2 72.1 all-gather.4

commit v3 on v2

--- a/solution.py
+++ b/solution.py
@@ -41,7 +41,7 @@
 NEAR = (0, 2, 6, 4)
 
 
-def node_sum(sent, kept, nodes, waits):
+def node_first(sent, kept, nodes, waits):
     half, f = sent.shape[0] // 2, sent.shape[1] // 4
     came = swap(sent, 1, nodes)
 
@@ -50,12 +50,17 @@
         return add(kept[at], came[at])
 
     one_in, two_in = after((part(1, 3, True), part(2, 4, False)), *waits)
-    one_in, two_in = swap(one_in, 2, nodes), swap(two_in, 4, nodes)
-    one_out = swap(add(part(3, 4, True), one_in[:, f:]), 4, nodes)
-    two_out = swap(add(part(1, 2, False), two_in[:, :f]), 2, nodes)
+    return part, swap(one_in, 2, nodes), swap(two_in, 4, nodes)
+
+
+def node_second(part, one_in, two_in, nodes, waits):
+    f = one_in.shape[1] // 2
+    one_out = after(add(part(3, 4, True), one_in[:, f:]), *waits)
+    two_out = after(add(part(1, 2, False), two_in[:, :f]), *waits)
+    one_out, two_out = swap(one_out, 4, nodes), swap(two_out, 2, nodes)
     one = add(add(part(0, 1, True), one_in[:, :f]), one_out)
     two = add(add(part(0, 1, False), two_in[:, f:]), two_out)
-    return (one, two), (one_in, two_in)
+    return (one, two), (one_out, two_out)
 
 
 def line_sum(terms, groups, waits):
@@ -67,7 +72,9 @@
         up_out, down_out = after((up_out, down_out), *waits[step - 1])
         up = up_line(up_out, range(min(step, groups - 1)))
         down = down_line(down_out, range(max(groups - step, 1), groups))
-    return add(terms[0].astype(jnp.float32) + up.astype(jnp.float32), down)
+        if step == 1:
+            first = (up, down)
+    return add(terms[0].astype(jnp.float32) + up.astype(jnp.float32), down), first
 
 
 def per_device(tokens, cotangent, gate_weight, up_weight, down_weight):
@@ -83,9 +90,6 @@
     order = shift_order(groups)
     share = rows // nodes
 
-    slices = jnp.stack(
-        [lax.dynamic_slice_in_dim(a, node * share, share, 0) for a in (tokens, cotangent)]
-    )
     def units(d):
         return d * owned
 
@@ -106,22 +110,18 @@
         ready[k] = (got,)
         gate_up = lax.dynamic_update_slice(gate_up, got, (((me - k) % groups) * depth, 0))
 
-    up_going = down_going = slices
-    ups, downs = [], []
-    for step in range(1, groups):
-        if step == groups - 1:
-            up_going, down_going = after((up_going, down_going), *ready[order[0]])
-        up_going = up_line(up_going, range(step - 1, groups - 1))
-        down_going = down_line(down_going, range(1, groups - step + 1))
-        ups.append(up_going)
-        downs.append(down_going)
-    arrived = [jnp.where(me >= k, ups[k - 1], downs[groups - k - 1]) for k in range(1, groups)]
+    shares = jnp.stack(
+        [lax.dynamic_slice_in_dim(a, node * share, share, 0) for a in (tokens, cotangent)]
+    )
+    lines = lax.all_gather(shares, "local")
+    lines = [
+        lax.dynamic_index_in_dim(lines, (me - k) % groups, 0, keepdims=False)
+        for k in range(1, groups)
+    ]
+    came = [ready[k][0] for k in order]
     tok_rest, cot_rest = (
         lax.all_gather(
-            after(jnp.concatenate([a[i] for a in arrived], 0), *ready[order[1 + i]]),
-            "node",
-            axis=0,
-            tiled=True,
+            after(jnp.concatenate([a[i] for a in lines], 0), *came), "node", axis=0, tiled=True
         )
         for i in (0, 1)
     )
@@ -190,12 +190,15 @@
         return dot(both_rows, weights, ((1,), (1,))).astype(jnp.bfloat16)
 
     near_known = nodes == 8
-    hidden_rows = by_block(*hiddens)
+    hidden_rows = by_block(*after(tuple(hiddens), *down_terms.values()))
     if near_known:
         out_first = out_sent = out_term(near(down, 1, 1))
         out_kept = out_term(near(down, 1, 0))
+        out_state = node_first(out_sent, out_kept, nodes, ready[order[0]])
+        moved = out_state[1:]
     else:
         out_first = out_term(down)
+        moved = ()
 
     down_then = after(down, out_first)
     backs = [dot(c, down_then, ((1,), (1,))) for c in cots]
@@ -209,39 +212,18 @@
     gate_up_terms = {
         order[0]: summed([columns(t, order[0]) for t in toks], both).astype(jnp.bfloat16)
     }
-    both_rows = after(by_block(*both), gate_up_terms[order[0]])
+    passed = [ready[k][0] for k in order]
+    both_rows = after(by_block(*both), gate_up_terms[order[0]], *passed, *moved)
     if near_known:
         in_first = in_sent = in_term(near(gate_up, 0, 1))
-        in_kept = in_term(near(gate_up, 0, 0))
     else:
         in_first = in_term(gate_up)
     both = after(tuple(both), in_first)
     for k in order[1:]:
         gate_up_terms[k] = summed([columns(t, k) for t in toks], both).astype(jnp.bfloat16)
-
-    passed = [ready[k][0] for k in order]
-    if near_known:
-        out_sums, came = node_sum(out_sent, out_kept, nodes, passed)
-        in_sums, _ = node_sum(in_sent, in_kept, nodes, came)
-    else:
-        out_sums, in_sums = (
-            jnp.split(
-                lax.psum_scatter(t, "node", scatter_dimension=1, tiled=True), 2, 0
-            )
-            for t in (out_first, in_first)
-        )
-
-    gate_grad = jnp.zeros((depth, unit_count), jnp.float32)
-    up_grad = jnp.zeros((depth, unit_count), jnp.float32)
-    for k in order:
-        ready[k] = (shift(after(gate_up_terms[k], *ready[k]), k, groups),)
-        got = ready[k][0].astype(jnp.float32)
-        at = (0, units((me - k) % groups))
-        gate_grad = lax.dynamic_update_slice(gate_grad, got[:, :owned], at)
-        up_grad = lax.dynamic_update_slice(up_grad, got[:, owned:], at)
-    term = summed([columns(t, 0) for t in toks], both)
-    gate_grad = lax.dynamic_update_slice(gate_grad, term[:, :owned], (0, units(me)))
-    up_grad = lax.dynamic_update_slice(up_grad, term[:, owned:], (0, units(me)))
+    if near_known:
+        both_rows = after(both_rows, *gate_up_terms.values())
+        in_kept = in_term(near(gate_up, 0, 0))
 
     def finish(halves, waits):
         terms = {}
@@ -250,8 +232,36 @@
             terms[k] = halves[2 * i // groups][at * rows : (at + 1) * rows]
         return line_sum(terms, groups, waits)
 
-    block_out = finish(out_sums, [()] * groups)
-    input_grad = finish(in_sums, [ready[k] for k in order])
+    gate_grad = jnp.zeros((depth, unit_count), jnp.float32)
+    up_grad = jnp.zeros((depth, unit_count), jnp.float32)
+    for k in order:
+        ready[k] = (shift(after(gate_up_terms[k], *ready[k]), k, groups),)
+        got = ready[k][0].astype(jnp.float32)
+        at = (0, units((me - k) % groups))
+        gate_grad = lax.dynamic_update_slice(gate_grad, got[:, :owned], at)
+        up_grad = lax.dynamic_update_slice(up_grad, got[:, owned:], at)
+    if near_known:
+        out_sums, _ = node_second(*out_state, nodes, ())
+        block_out, _ = finish(out_sums, [()] * groups)
+        in_state = node_first(in_sent, in_kept, nodes, ())
+        in_sums, _ = node_second(*in_state, nodes, ())
+        waits = [[ready[k][0] for k in order]] + [()] * (groups - 1)
+        input_grad, _ = finish(in_sums, waits)
+    else:
+        block_out, input_grad = (
+            finish(
+                jnp.split(
+                    lax.psum_scatter(t, "node", scatter_dimension=1, tiled=True), 2, 0
+                ),
+                [()] * groups,
+            )[0]
+            for t in (out_first, in_first)
+        )
+
+    term = summed([columns(t, 0) for t in toks], both)
+    gate_grad = lax.dynamic_update_slice(gate_grad, term[:, :owned], (0, units(me)))
+    up_grad = lax.dynamic_update_slice(up_grad, term[:, owned:], (0, units(me)))
+
     return (block_out, input_grad, gate_grad, up_grad, down_grad)
 
 

time: 746 us -> 689 us (0.924)
  waiting for transfers between devices: 382 us -> 322 us
  other arithmetic: 47.9 us -> 59.6 us
  starting transfers between devices: 103 us -> 92.8 us
    ppermute x15, waiting for transfers between devices: 270 us -> 99.1 us  [shift(): lax.ppermute(value, 'local', [(i, (i + step) % groups) for i in range(gro...]
    all_gather x2 -> x3, waiting for transfers between devices: 7.43 us -> 153 us  [the longest x1 132 us: per_device(): lines = lax.all_gather(shares, 'local')]
    ppermute x9 -> x6, waiting for transfers between devices: 22.9 us -> 2.79 us  [down_line(): return lax.ppermute(value, 'local', [(i, i - 1) for i in senders])]
    ppermute x9 -> x6, waiting for transfers between devices: 45 us -> 31.7 us  [up_line(): return lax.ppermute(value, 'local', [(i, i + 1) for i in senders])]
    ppermute x9 -> x6, starting transfers between devices: 32.6 us -> 25.2 us  [up_line(): return lax.ppermute(value, 'local', [(i, i + 1) for i in senders])]
  transfers between devices with their start and end apart: 45 -> 40, of which waited for: 21 -> 19; matrix products, arithmetic and copies ran while one was open for 28% -> 30% of each run, Pallas kernels for 0% -> 0%
where the time goes in v3:
time: 689 us; the launch traced here: 680 us
  waiting for transfers between devices  322 us (47%)
  matrix products  128 us (19%)
  starting transfers between devices  92.8 us (13%)
  local copies, waits for them, and re-layouts  63.6 us (9%)
  other arithmetic  59.6 us (9%)
  between operations  15 us (2%)
    all_gather x1, waiting for transfers between devices, per_device(): lines = lax.all_gather(shares, 'local')  132 us
    dot_general x24, matrix products, dot(): lax.dot_general(left, right, (dims, ((), ())), preferred_element_type=jnp...  128 us
    ppermute x15, waiting for transfers between devices, shift(): lax.ppermute(value, 'local', [(i, (i + step) % groups) for i in range(gro...  99.1 us
    ppermute x15, starting transfers between devices, shift(): lax.ppermute(value, 'local', [(i, (i + step) % groups) for i in range(gro...  54.5 us
    ppermute x10, waiting for transfers between devices, swap(): return lax.ppermute(value, 'node', [(i, i ^ bit) for i in range(nodes)])  35.2 us
    ppermute x6, waiting for transfers between devices, up_line(): return lax.ppermute(value, 'local', [(i, i + 1) for i in senders])  31.7 us
    convert_element_type x14, other arithmetic, add(): return (a.astype(jnp.float32) + b.astype(jnp.float32)).astype(jnp.bfloat16)  31.7 us
    ppermute x6, starting transfers between devices, up_line(): return lax.ppermute(value, 'local', [(i, i + 1) for i in senders])  25.2 us
  transfers between devices with their start and end apart: 40, of which 19 were waited for; matrix products, arithmetic and copies ran while one was open for 30% of the time, Pallas kernels for 0%

profile of v3, /device:TPU:0, one launch (start us, length us, event | category | flops | bytes accessed | tf_op | source)
XLA Modules:
  0.0 680.1 jit_solution(9968988202451588831)
XLA Ops:
  19.2 132.3 %all-gather.9.cloned.1.call-done = bf16[8,64,4096]{2,1,0:T(8,128)(2,1)} async-done(((bf16[2,64,4096]{2,1,0:T(8,128)(2,1)}), bf16[8,64,4096]{2,1,0:T(8,128)(2,1)}) %all-gather.9.cloned.1.call-update) | async-done | bytes 4194320 | tf_op jit(solution)/shard_map/all_gather | solution.py:116
  172.8 43.4 %collective-permute-done.3 = bf16[1024,384]{1,0:T(8,128)(2,1)} collective-permute-done((bf16[1024,384]{1,0:T(8,128)(2,1)}, bf16[1024,384]{1,0:T(8,128)(2,1)}, u32[]{:S(2)}, u32[]{:S(2)}) %collective-permute-start.3) | collective-permute-done | bytes 786464 | tf_op jit(solution)/shard_map/ppermute | solution.py:18
  216.1 30.7 %collective-permute-start.7 = (bf16[384,1024]{1,0:T(8,128)(2,1)}, bf16[384,1024]{1,0:T(8,128)(2,1)}, u32[]{:S(2)}, u32[]{:S(2)}) collective-permute-start(bf16[384,1024]{1,0:T(8,128)(2,1)} %get-tuple-element.54), channel_id=1, source_target_pairs={{0,1},{1,2},{2,3},{3,0},{4,5},{5,6},{6,7},{7,4},{8,9},{9,10},{10,1... | collective-permute-start | bytes 2359304 | tf_op jit(solution)/shard_map/ppermute | solution.py:18
  263.4 16.2 %fusion.106 = f32[1536,768]{0,1:T(8,128)S(1)} fusion(bf16[1536,4096]{1,0:T(8,128)(2,1)} %all-gather.5.cloned.1.call-done, bf16[4096,768]{1,0:T(8,128)(2,1)} %copy-done), kind=kOutput, calls=%fused_computation.209 | convolution fusion | flops 9663676416 | bytes 23592960 | tf_op jit(solution)/shard_map/dot_general | solution.py:10
  283.5 20.4 %all-gather.7.cloned.1.call-done = bf16[1536,4096]{1,0:T(8,128)(2,1)} async-done(((bf16[192,4096]{1,0:T(8,128)(2,1)}), bf16[1536,4096]{1,0:T(8,128)(2,1)}) %all-gather.7.cloned.1.call-update) | async-done | bytes 12582928 | tf_op jit(solution)/shard_map/all_gather | solution.py:123
  303.9 5.2 multiply_convert_fusion.8
  332.3 7.4 %convolution_convert_fusion.2 = bf16[2048,2048]{1,0:T(8,128)(2,1)} fusion(bf16[384,512]{1,0:T(8,128)(2,1)S(1)} %get-tuple-element.116, bf16[384,512]{1,0:T(8,128)(2,1)S(1)} %get-tuple-element.117, bf16[384,512]{1,0:T(8,128)(2,1)S(1)} %get-tuple-element.118, bf16[384,512]{1,0:T(8,128)(2,1)S(1)} %get-tuple-element.119, bf16[512,384]{0,1:T(8,128)(2,1)S(1)} %copy-done.40, ...), kind=kOutput, calls=%fused_computation.2 | convolution fusion | flops 3238002688 | bytes 11534336 | tf_op jit(solution)/shard_map/dot_general | solution.py:10
  345.0 8.7 %multiply_convert_fusion.4 = (bf16[1536,384]{0,1:T(8,128)(2,1)S(1)}, bf16[1536,384]{0,1:T(8,128)(2,1)S(1)}) fusion(f32[1536,768]{0,1:T(8,128)S(1)} %bitcast.61, bf16[1536,4096]{1,0:T(8,128)(2,1)} %all-gather.7.cloned.1.call-done, bf16[384,4096]{1,0:T(8,128)(2,1)S(1)} %constant_dynamic-update-slice_fusion), kind=kOutput, calls=%fused_computation.45 | convolution fusion | flops 4839505920 | bytes 22806528 | tf_op jit(solution)/shard_map/dot_general | solution.py:10
  353.7 7.2 %convolution_convert_fusion.3 = bf16[2048,2048]{1,0:T(8,128)(2,1)} fusion(bf16[384,512]{1,0:T(8,128)(2,1)S(1)} %get-tuple-element.120, bf16[384,512]{1,0:T(8,128)(2,1)S(1)} %get-tuple-element.121, bf16[384,512]{1,0:T(8,128)(2,1)S(1)} %get-tuple-element.122, bf16[384,512]{1,0:T(8,128)(2,1)S(1)} %get-tuple-element.115, bf16[512,384]{0,1:T(8,128)(2,1)S(1)} %copy-done.40, ...), kind=kOutput, calls=%fused_computation.3 | convolution fusion | flops 3238002688 | bytes 11534336 | tf_op jit(solution)/shard_map/dot_general | solution.py:10
  366.7 5.9 add_convert_fusion.2
  372.5 7.8 %collective-permute-done.10 = bf16[384,1024]{1,0:T(8,128)(2,1)} collective-permute-done((bf16[384,1024]{1,0:T(8,128)(2,1)}, bf16[384,1024]{1,0:T(8,128)(2,1)}, u32[]{:S(2)}, u32[]{:S(2)}) %collective-permute-start.10) | collective-permute-done | bytes 786464 | tf_op jit(solution)/shard_map/ppermute | solution.py:18
  399.7 8.8 %pad_maximum_fusion = bf16[2048,768]{0,1:T(8,128)(2,1)S(1)} fusion(bf16[512,768]{0,1:T(8,128)(2,1)S(1)} %copy-done.11, bf16[512,384]{0,1:T(8,128)(2,1)S(1)} %get-tuple-element.137, bf16[512,384]{0,1:T(8,128)(2,1)S(1)} %get-tuple-element.136, bf16[512,768]{0,1:T(8,128)(2,1)S(1)} %copy-done.12, bf16[512,768]{0,1:T(8,128)(2,1)S(1)} %copy-done.13), kind=kLoop, calls=%fused_computation.8 | loop fusion | flops 15728640 | bytes 6291456 | tf_op jit(solution)/shard_map/concatenate | solution.py:175
  411.0 5.9 multiply_convert_fusion.2
  416.9 10.6 %collective-permute-done.22 = bf16[384,1024]{1,0:T(8,128)(2,1)} collective-permute-done((bf16[384,1024]{1,0:T(8,128)(2,1)}, bf16[384,1024]{1,0:T(8,128)(2,1)}, u32[]{:S(2)}, u32[]{:S(2)}) %collective-permute-start.22) | collective-permute-done | bytes 786464 | tf_op jit(solution)/shard_map/ppermute | solution.py:18
  428.3 11.4 %convolution_convert_fusion.1 = bf16[2048,2048]{1,0:T(8,128)(2,1)} fusion(bf16[2048,768]{0,1:T(8,128)(2,1)S(1)} %pad_maximum_fusion, bf16[512,768]{1,0:T(8,128)(2,1)S(1)} %copy-done.34, bf16[512,768]{1,0:T(8,128)(2,1)S(1)} %copy-done.35, bf16[512,768]{1,0:T(8,128)(2,1)S(1)} %copy-done.36, bf16[512,768]{1,0:T(8,128)(2,1)S(1)} %copy-done.37), kind=kOutput, calls=%fused_computation.1 | convolution fusion | flops 6459228160 | bytes 14680064 | tf_op jit(solution)/shard_map/dot_general | solution.py:10
  446.5 5.8 multiply_convert_fusion.1
  452.3 5.9 multiply_convert_fusion
  458.2 9.4 %convolution_convert_fusion = bf16[2048,2048]{1,0:T(8,128)(2,1)S(1)} fusion(bf16[2048,768]{0,1:T(8,128)(2,1)S(1)} %pad_maximum_fusion, bf16[512,768]{1,0:T(8,128)(2,1)S(1)} %copy-done.31, bf16[512,768]{1,0:T(8,128)(2,1)S(1)} %copy-done.32, bf16[512,768]{1,0:T(8,128)(2,1)S(1)} %copy-done.33, bf16[512,768]{1,0:T(8,128)(2,1)S(1)} %copy-done.30), kind=kOutput, calls=%fused_computation | convolution fusion | flops 6459228160 | bytes 14680064 | tf_op jit(solution)/shard_map/dot_general | solution.py:10
  487.4 25.3 %collective-permute-done.28 = bf16[1024,768]{1,0:T(8,128)(2,1)} collective-permute-done((bf16[1024,768]{1,0:T(8,128)(2,1)}, bf16[1024,768]{1,0:T(8,128)(2,1)}, u32[]{:S(2)}, u32[]{:S(2)}) %collective-permute-start.28) | collective-permute-done | bytes 1572896 | tf_op jit(solution)/shard_map/ppermute | solution.py:18
  533.5 18.3 %collective-permute-done.12 = bf16[1024,512]{1,0:T(8,128)(2,1)} collective-permute-done((bf16[1024,512]{1,0:T(8,128)(2,1)S(1)}, bf16[1024,512]{1,0:T(8,128)(2,1)}, u32[]{:S(2)}, u32[]{:S(2)}) %collective-permute-start.12) | collective-permute-done | bytes 1048608 | tf_op jit(solution)/shard_map/ppermute | solution.py:38
  551.8 4.7 add_convert_fusion.19
  558.4 14.9 %collective-permute-done.25 = bf16[1024,512]{1,0:T(8,128)(2,1)} collective-permute-done((bf16[1024,512]{1,0:T(8,128)(2,1)}, bf16[1024,512]{1,0:T(8,128)(2,1)}, u32[]{:S(2)}, u32[]{:S(2)}) %collective-permute-start.25) | collective-permute-done | bytes 1048608 | tf_op jit(solution)/shard_map/ppermute | solution.py:38
  577.2 6.3 add_multiply_fusion
  585.1 12.0 %collective-permute-done.30 = bf16[1024,768]{1,0:T(8,128)(2,1)} collective-permute-done((bf16[1024,768]{1,0:T(8,128)(2,1)}, bf16[1024,768]{1,0:T(8,128)(2,1)}, u32[]{:S(2)}, u32[]{:S(2)}) %collective-permute-start.30) | collective-permute-done | bytes 1572896 | tf_op jit(solution)/shard_map/ppermute | solution.py:18
  610.8 6.4 collective-permute-done.15
  618.2 5.0 collective-permute-start.17
  623.2 5.2 collective-permute-done.31
  629.4 5.0 collective-permute-start.33
  634.8 4.8 collective-permute-done.17
  641.3 5.0 collective-permute-start.19
  652.5 5.0 collective-permute-start.35
  665.9 6.5 collective-permute-done.35
  (253 shorter events, 197.9 us)
Async XLA Ops:
  7.2 144.3 %all-gather.9.cloned.1.call-start = ((), (), s32[]{:S(2)}) async-start(), calls=%async_computation.2 | async-start | bytes 5242880 | tf_op jit(solution)/shard_map/all_gather | solution.py:116
  9.7 253.6 %all-gather.5.cloned.1.call-start = ((), (), s32[]{:S(2)}) async-start(), calls=%async_computation | async-start | bytes 14155776 | tf_op jit(solution)/shard_map/all_gather | solution.py:123
  11.3 144.4 %collective-permute-start = (bf16[1024,384]{1,0:T(8,128)(2,1)}, bf16[1024,384]{1,0:T(8,128)(2,1)}, u32[]{:S(2)}, u32[]{:S(2)}) collective-permute-start(bf16[1024,384]{1,0:T(8,128)(2,1)} %get-tuple-element.132), channel_id=1, source_target_pairs={{0,2},{1,3},{2,0},{3,1},{4,6},{5,7},{6,4},{7,5},{8,10},{9,11},{10,... | collective-permute-start | bytes 2359304 | tf_op jit(solution)/shard_map/ppermute | solution.py:18
  15.4 140.4 %collective-permute-start.1 = (bf16[1024,384]{1,0:T(8,128)(2,1)}, bf16[1024,384]{1,0:T(8,128)(2,1)}, u32[]{:S(2)}, u32[]{:S(2)}) collective-permute-start(bf16[1024,384]{1,0:T(8,128)(2,1)} %get-tuple-element.131), channel_id=1, source_target_pairs={{0,1},{1,2},{2,3},{3,0},{4,5},{5,6},{6,7},{7,4},{8,9},{9,10},{10,1... | collective-permute-start | bytes 2359304 | tf_op jit(solution)/shard_map/ppermute | solution.py:18
  17.0 138.8 %collective-permute-start.2 = (bf16[1024,384]{1,0:T(8,128)(2,1)}, bf16[1024,384]{1,0:T(8,128)(2,1)}, u32[]{:S(2)}, u32[]{:S(2)}) collective-permute-start(bf16[1024,384]{1,0:T(8,128)(2,1)} %get-tuple-element.130), channel_id=1, source_target_pairs={{0,3},{1,0},{2,1},{3,2},{4,7},{5,4},{6,5},{7,6},{8,11},{9,8},{10,9... | collective-permute-start | bytes 2359304 | tf_op jit(solution)/shard_map/ppermute | solution.py:18
  155.8 148.1 %all-gather.7.cloned.1.call-start = ((), (), s32[]{:S(2)}) async-start(), calls=%async_computation.1 | async-start | bytes 14155776 | tf_op jit(solution)/shard_map/all_gather | solution.py:123
  160.2 55.9 %collective-permute-start.3 = (bf16[1024,384]{1,0:T(8,128)(2,1)}, bf16[1024,384]{1,0:T(8,128)(2,1)}, u32[]{:S(2)}, u32[]{:S(2)}) collective-permute-start(bf16[1024,384]{1,0:T(8,128)(2,1)} %get-tuple-element.45), channel_id=1, source_target_pairs={{0,2},{1,3},{2,0},{3,1},{4,6},{5,7},{6,4},{7,5},{8,10},{9,11},{10,... | collective-permute-start | bytes 2359304 | tf_op jit(solution)/shard_map/ppermute | solution.py:18
  160.2 55.9 %collective-permute-start.4 = (bf16[1024,384]{1,0:T(8,128)(2,1)}, bf16[1024,384]{1,0:T(8,128)(2,1)}, u32[]{:S(2)}, u32[]{:S(2)}) collective-permute-start(bf16[1024,384]{1,0:T(8,128)(2,1)} %get-tuple-element.46), channel_id=1, source_target_pairs={{0,1},{1,2},{2,3},{3,0},{4,5},{5,6},{6,7},{7,4},{8,9},{9,10},{10,1... | collective-permute-start | bytes 2359304 | tf_op jit(solution)/shard_map/ppermute | solution.py:18
  164.4 82.5 %collective-permute-start.5 = (bf16[1024,384]{1,0:T(8,128)(2,1)}, bf16[1024,384]{1,0:T(8,128)(2,1)}, u32[]{:S(2)}, u32[]{:S(2)}) collective-permute-start(bf16[1024,384]{1,0:T(8,128)(2,1)} %get-tuple-element.47), channel_id=1, source_target_pairs={{0,3},{1,0},{2,1},{3,2},{4,7},{5,4},{6,5},{7,6},{8,11},{9,8},{10,9... | collective-permute-start | bytes 2359304 | tf_op jit(solution)/shard_map/ppermute | solution.py:18
  216.1 101.5 %collective-permute-start.6 = (bf16[384,1024]{1,0:T(8,128)(2,1)}, bf16[384,1024]{1,0:T(8,128)(2,1)}, u32[]{:S(2)}, u32[]{:S(2)}) collective-permute-start(bf16[384,1024]{1,0:T(8,128)(2,1)} %get-tuple-element.52), channel_id=1, source_target_pairs={{0,2},{1,3},{2,0},{3,1},{4,6},{5,7},{6,4},{7,5},{8,10},{9,11},{10,... | collective-permute-start | bytes 2359304 | tf_op jit(solution)/shard_map/ppermute | solution.py:18
  216.1 101.5 %collective-permute-start.7 = (bf16[384,1024]{1,0:T(8,128)(2,1)}, bf16[384,1024]{1,0:T(8,128)(2,1)}, u32[]{:S(2)}, u32[]{:S(2)}) collective-permute-start(bf16[384,1024]{1,0:T(8,128)(2,1)} %get-tuple-element.54), channel_id=1, source_target_pairs={{0,1},{1,2},{2,3},{3,0},{4,5},{5,6},{6,7},{7,4},{8,9},{9,10},{10,1... | collective-permute-start | bytes 2359304 | tf_op jit(solution)/shard_map/ppermute | solution.py:18
  246.8 70.8 %collective-permute-start.8 = (bf16[384,1024]{1,0:T(8,128)(2,1)}, bf16[384,1024]{1,0:T(8,128)(2,1)}, u32[]{:S(2)}, u32[]{:S(2)}) collective-permute-start(bf16[384,1024]{1,0:T(8,128)(2,1)} %get-tuple-element.56), channel_id=1, source_target_pairs={{0,3},{1,0},{2,1},{3,2},{4,7},{5,4},{6,5},{7,6},{8,11},{9,8},{10,9... | collective-permute-start | bytes 2359304 | tf_op jit(solution)/shard_map/ppermute | solution.py:18
  339.7 27.0 %collective-permute-start.9 = (bf16[2048,2048]{1,0:T(8,128)(2,1)}, bf16[2048,2048]{1,0:T(8,128)(2,1)}, u32[]{:S(2)}, u32[]{:S(2)}) collective-permute-start(bf16[2048,2048]{1,0:T(8,128)(2,1)} %convolution_convert_fusion.2), channel_id=1, source_target_pairs={{0,4},{4,0},{8,12},{12,8},{16,20},{20,16},{24,28},{28,24},{1,5},{5... | collective-permute-start | bytes 25165832 | tf_op jit(solution)/shard_map/ppermute | solution.py:38
  342.6 37.8 %collective-permute-start.10 = (bf16[384,1024]{1,0:T(8,128)(2,1)}, bf16[384,1024]{1,0:T(8,128)(2,1)}, u32[]{:S(2)}, u32[]{:S(2)}) collective-permute-start(bf16[384,1024]{1,0:T(8,128)(2,1)} %multiply_convert_fusion.8), channel_id=1, source_target_pairs={{0,2},{1,3},{2,0},{3,1},{4,6},{5,7},{6,4},{7,5},{8,10},{9,11},{10,... | collective-permute-start | bytes 2359304 | tf_op jit(solution)/shard_map/ppermute | solution.py:18
  380.3 47.3 %collective-permute-start.11 = (bf16[1024,1024]{1,0:T(8,128)(2,1)}, bf16[1024,1024]{1,0:T(8,128)(2,1)}, u32[]{:S(2)}, u32[]{:S(2)}) collective-permute-start(bf16[1024,1024]{1,0:T(8,128)(2,1)} %get-tuple-element.59), channel_id=1, source_target_pairs={{0,16},{4,20},{8,24},{12,28},{16,0},{20,4},{24,8},{28,12},{1,17},{... | collective-permute-start | bytes 6291464 | tf_op jit(solution)/shard_map/ppermute | solution.py:38
  381.3 47.0 %collective-permute-start.13 = (bf16[1024,1024]{1,0:T(8,128)(2,1)}, bf16[1024,1024]{1,0:T(8,128)(2,1)}, u32[]{:S(2)}, u32[]{:S(2)}) collective-permute-start(bf16[1024,1024]{1,0:T(8,128)(2,1)} %get-tuple-element.60), channel_id=1, source_target_pairs={{0,8},{4,12},{8,0},{12,4},{16,24},{20,28},{24,16},{28,20},{1,9},{5... | collective-permute-start | bytes 6291464 | tf_op jit(solution)/shard_map/ppermute | solution.py:38
  390.8 26.1 %collective-permute-start.21 = (bf16[384,1024]{1,0:T(8,128)(2,1)}, bf16[384,1024]{1,0:T(8,128)(2,1)}, u32[]{:S(2)}, u32[]{:S(2)}) collective-permute-start(bf16[384,1024]{1,0:T(8,128)(2,1)} %multiply_convert_fusion.7), channel_id=1, source_target_pairs={{0,1},{1,2},{2,3},{3,0},{4,5},{5,6},{6,7},{7,4},{8,9},{9,10},{10,1... | collective-permute-start | bytes 2359304 | tf_op jit(solution)/shard_map/ppermute | solution.py:18
  391.3 36.2 %collective-permute-start.22 = (bf16[384,1024]{1,0:T(8,128)(2,1)}, bf16[384,1024]{1,0:T(8,128)(2,1)}, u32[]{:S(2)}, u32[]{:S(2)}) collective-permute-start(bf16[384,1024]{1,0:T(8,128)(2,1)} %multiply_convert_fusion.6), channel_id=1, source_target_pairs={{0,3},{1,0},{2,1},{3,2},{4,7},{5,4},{6,5},{7,6},{8,11},{9,8},{10,9... | collective-permute-start | bytes 2359304 | tf_op jit(solution)/shard_map/ppermute | solution.py:18
  439.7 28.0 %collective-permute-start.23 = (bf16[2048,2048]{1,0:T(8,128)(2,1)}, bf16[2048,2048]{1,0:T(8,128)(2,1)}, u32[]{:S(2)}, u32[]{:S(2)}) collective-permute-start(bf16[2048,2048]{1,0:T(8,128)(2,1)} %convolution_convert_fusion.1), channel_id=1, source_target_pairs={{0,4},{4,0},{8,12},{12,8},{16,20},{20,16},{24,28},{28,24},{1,5},{5... | collective-permute-start | bytes 25165832 | tf_op jit(solution)/shard_map/ppermute | solution.py:38
  440.9 71.8 %collective-permute-start.28 = (bf16[1024,768]{1,0:T(8,128)(2,1)}, bf16[1024,768]{1,0:T(8,128)(2,1)}, u32[]{:S(2)}, u32[]{:S(2)}) collective-permute-start(bf16[1024,768]{1,0:T(8,128)(2,1)} %multiply_convert_fusion.2), channel_id=1, source_target_pairs={{0,2},{1,3},{2,0},{3,1},{4,6},{5,7},{6,4},{7,5},{8,10},{9,11},{10,... | collective-permute-start | bytes 4718600 | tf_op jit(solution)/shard_map/ppermute | solution.py:18
  472.1 47.8 %collective-permute-start.24 = (bf16[1024,1024]{1,0:T(8,128)(2,1)S(1)}, bf16[1024,1024]{1,0:T(8,128)(2,1)S(1)}, u32[]{:S(2)}, u32[]{:S(2)}) collective-permute-start(bf16[1024,1024]{1,0:T(8,128)(2,1)S(1)} %get-tuple-element.74), channel_id=1, source_target_pairs={{0,16},{4,20},{8,24},{12,28},{16,0},{20,4},{24,8},{28,12},{1,17},{... | collective-permute-start | bytes 6291464 | tf_op jit(solution)/shard_map/ppermute | solution.py:38
  480.4 76.6 %collective-permute-start.26 = (bf16[1024,1024]{1,0:T(8,128)(2,1)}, bf16[1024,1024]{1,0:T(8,128)(2,1)S(1)}, u32[]{:S(2)}, u32[]{:S(2)}) collective-permute-start(bf16[1024,1024]{1,0:T(8,128)(2,1)} %get-tuple-element.75), channel_id=1, source_target_pairs={{0,8},{4,12},{8,0},{12,4},{16,24},{20,28},{24,16},{28,20},{1,9},{5... | collective-permute-start | bytes 6291464 | tf_op jit(solution)/shard_map/ppermute | solution.py:38
  516.4 35.3 %collective-permute-start.12 = (bf16[1024,512]{1,0:T(8,128)(2,1)S(1)}, bf16[1024,512]{1,0:T(8,128)(2,1)}, u32[]{:S(2)}, u32[]{:S(2)}) collective-permute-start(bf16[1024,512]{1,0:T(8,128)(2,1)S(1)} %add_convert_fusion.20), channel_id=1, source_target_pairs={{0,8},{4,12},{8,0},{12,4},{16,24},{20,28},{24,16},{28,20},{1,9},{5... | collective-permute-start | bytes 3145736 | tf_op jit(solution)/shard_map/ppermute | solution.py:38
  523.3 49.9 %collective-permute-start.25 = (bf16[1024,512]{1,0:T(8,128)(2,1)}, bf16[1024,512]{1,0:T(8,128)(2,1)}, u32[]{:S(2)}, u32[]{:S(2)}) collective-permute-start(bf16[1024,512]{1,0:T(8,128)(2,1)} %add_convert_fusion.10), channel_id=1, source_target_pairs={{0,8},{4,12},{8,0},{12,4},{16,24},{20,28},{24,16},{28,20},{1,9},{5... | collective-permute-start | bytes 3145736 | tf_op jit(solution)/shard_map/ppermute | solution.py:38
  525.3 58.2 %collective-permute-start.29 = (bf16[1024,768]{1,0:T(8,128)(2,1)}, bf16[1024,768]{1,0:T(8,128)(2,1)}, u32[]{:S(2)}, u32[]{:S(2)}) collective-permute-start(bf16[1024,768]{1,0:T(8,128)(2,1)} %multiply_convert_fusion.1), channel_id=1, source_target_pairs={{0,1},{1,2},{2,3},{3,0},{4,5},{5,6},{6,7},{7,4},{8,9},{9,10},{10,1... | collective-permute-start | bytes 4718600 | tf_op jit(solution)/shard_map/ppermute | solution.py:18
  529.2 68.0 %collective-permute-start.30 = (bf16[1024,768]{1,0:T(8,128)(2,1)}, bf16[1024,768]{1,0:T(8,128)(2,1)}, u32[]{:S(2)}, u32[]{:S(2)}) collective-permute-start(bf16[1024,768]{1,0:T(8,128)(2,1)} %multiply_convert_fusion), channel_id=1, source_target_pairs={{0,3},{1,0},{2,1},{3,2},{4,7},{5,4},{6,5},{7,6},{8,11},{9,8},{10,9... | collective-permute-start | bytes 4718600 | tf_op jit(solution)/shard_map/ppermute | solution.py:18
  556.4 42.5 %collective-permute-start.14 = (bf16[1024,512]{1,0:T(8,128)(2,1)}, bf16[1024,512]{1,0:T(8,128)(2,1)}, u32[]{:S(2)}, u32[]{:S(2)}) collective-permute-start(bf16[1024,512]{1,0:T(8,128)(2,1)} %get-tuple-element.90), channel_id=1, source_target_pairs={{0,16},{4,20},{8,24},{12,28},{16,0},{20,4},{24,8},{28,12},{1,17},{... | collective-permute-start | bytes 3145736 | tf_op jit(solution)/shard_map/ppermute | solution.py:38
  576.6 28.4 %collective-permute-start.27 = (bf16[1024,512]{1,0:T(8,128)(2,1)S(1)}, bf16[1024,512]{1,0:T(8,128)(2,1)S(1)}, u32[]{:S(2)}, u32[]{:S(2)}) collective-permute-start(bf16[1024,512]{1,0:T(8,128)(2,1)S(1)} %get-tuple-element.86), channel_id=1, source_target_pairs={{0,16},{4,20},{8,24},{12,28},{16,0},{20,4},{24,8},{28,12},{1,17},{... | collective-permute-start | bytes 3145736 | tf_op jit(solution)/shard_map/ppermute | solution.py:38
  607.8 20.6 %collective-permute-start.31 = (bf16[512,512]{1,0:T(8,128)(2,1)S(1)}, bf16[512,512]{1,0:T(8,128)(2,1)S(1)}, u32[]{:S(2)}, u32[]{:S(2)}) collective-permute-start(bf16[512,512]{1,0:T(8,128)(2,1)S(1)} %get-tuple-element.79), channel_id=1, source_target_pairs={{0,1},{4,5},{8,9},{12,13},{16,17},{20,21},{24,25},{28,29}} | collective-permute-start | bytes 1572872 | tf_op jit(solution)/shard_map/ppermute | solution.py:22
  618.2 21.5 %collective-permute-start.17 = (bf16[512,512]{1,0:T(8,128)(2,1)S(1)}, bf16[512,512]{1,0:T(8,128)(2,1)S(1)}, u32[]{:S(2)}, u32[]{:S(2)}) collective-permute-start(bf16[512,512]{1,0:T(8,128)(2,1)S(1)} %get-tuple-element.63), channel_id=1, source_target_pairs={{0,1},{1,2},{4,5},{5,6},{8,9},{9,10},{12,13},{13,14},{16,17},{17,1... | collective-permute-start | bytes 1572872 | tf_op jit(solution)/shard_map/ppermute | solution.py:22
  629.4 21.5 %collective-permute-start.33 = (bf16[512,512]{1,0:T(8,128)(2,1)S(1)}, bf16[512,512]{1,0:T(8,128)(2,1)S(1)}, u32[]{:S(2)}, u32[]{:S(2)}) collective-permute-start(bf16[512,512]{1,0:T(8,128)(2,1)S(1)} %get-tuple-element.81), channel_id=1, source_target_pairs={{0,1},{1,2},{4,5},{5,6},{8,9},{9,10},{12,13},{13,14},{16,17},{17,1... | collective-permute-start | bytes 1572872 | tf_op jit(solution)/shard_map/ppermute | solution.py:22
  641.3 20.9 %collective-permute-start.19 = (bf16[512,512]{1,0:T(8,128)(2,1)S(1)}, bf16[512,512]{1,0:T(8,128)(2,1)S(1)}, u32[]{:S(2)}, u32[]{:S(2)}) collective-permute-start(bf16[512,512]{1,0:T(8,128)(2,1)S(1)} %get-tuple-element.65), channel_id=1, source_target_pairs={{0,1},{1,2},{2,3},{4,5},{5,6},{6,7},{8,9},{9,10},{10,11},{12,13},{... | collective-permute-start | bytes 1572872 | tf_op jit(solution)/shard_map/ppermute | solution.py:22
  (61 other events, 623.4 us)
Sparse Core Ops, SparseCore 0:
  10.2 141.2 all-gather.8
  155.9 73.3 all-gather.4
  231.8 72.1 all-gather.6

commit v4 on v3

--- a/solution.py
+++ b/solution.py
@@ -27,7 +27,7 @@
 
 
 def shift_order(groups):
-    return sorted(range(1, groups), key=lambda k: -min(k, groups - k))
+    return sorted(range(1, groups), key=lambda k: min(k, groups - k))
 
 
 def add(a, b):

time: 689 us -> 729 us (1.058)
  waiting for transfers between devices: 322 us -> 396 us
  starting transfers between devices: 92.8 us -> 59.1 us
    ppermute x15, waiting for transfers between devices: 99.1 us -> 148 us  [shift(): lax.ppermute(value, 'local', [(i, (i + step) % groups) for i in range(gro...]
    ppermute x15, starting transfers between devices: 54.5 us -> 21.7 us  [shift(): lax.ppermute(value, 'local', [(i, (i + step) % groups) for i in range(gro...]
    ppermute x10, waiting for transfers between devices: 35.2 us -> 60.3 us  [swap(): return lax.ppermute(value, 'node', [(i, i ^ bit) for i in range(nodes)])]
  transfers between devices with their start and end apart: 40 -> 40, of which waited for: 19 -> 17; matrix products, arithmetic and copies ran while one was open for 30% -> 29% of each run, Pallas kernels for 0% -> 0%
where the time goes in v4:
time: 729 us; the launch traced here: 720 us
  waiting for transfers between devices  396 us (54%)
  matrix products  127 us (17%)
  local copies, waits for them, and re-layouts  63.7 us (9%)
  other arithmetic  59.6 us (8%)
  starting transfers between devices  59.1 us (8%)
  between operations  15 us (2%)
    ppermute x15, waiting for transfers between devices, shift(): lax.ppermute(value, 'local', [(i, (i + step) % groups) for i in range(gro...  148 us
    all_gather x1, waiting for transfers between devices, per_device(): lines = lax.all_gather(shares, 'local')  135 us
    dot_general x24, matrix products, dot(): lax.dot_general(left, right, (dims, ((), ())), preferred_element_type=jnp...  127 us
    ppermute x10, waiting for transfers between devices, swap(): return lax.ppermute(value, 'node', [(i, i ^ bit) for i in range(nodes)])  60.3 us
    ppermute x6, waiting for transfers between devices, up_line(): return lax.ppermute(value, 'local', [(i, i + 1) for i in senders])  33 us
    convert_element_type x14, other arithmetic, add(): return (a.astype(jnp.float32) + b.astype(jnp.float32)).astype(jnp.bfloat16)  31.7 us
    ppermute x6, starting transfers between devices, up_line(): return lax.ppermute(value, 'local', [(i, i + 1) for i in senders])  24.1 us
    ppermute x15, starting transfers between devices, shift(): lax.ppermute(value, 'local', [(i, (i + step) % groups) for i in range(gro...  21.7 us
  transfers between devices with their start and end apart: 40, of which 17 were waited for; matrix products, arithmetic and copies ran while one was open for 29% of the time, Pallas kernels for 0%

profile of v4, /device:TPU:0, one launch (start us, length us, event | category | flops | bytes accessed | tf_op | source)
XLA Modules:
  0.0 720.5 jit_solution(10086858692198026536)
XLA Ops:
  17.4 135.1 %all-gather.9.cloned.1.call-done = bf16[8,64,4096]{2,1,0:T(8,128)(2,1)} async-done(((bf16[2,64,4096]{2,1,0:T(8,128)(2,1)}), bf16[8,64,4096]{2,1,0:T(8,128)(2,1)}) %all-gather.9.cloned.1.call-update) | async-done | bytes 4194320 | tf_op jit(solution)/shard_map/all_gather | solution.py:116
  173.5 10.3 %collective-permute-done.3 = bf16[1024,384]{1,0:T(8,128)(2,1)} collective-permute-done((bf16[1024,384]{1,0:T(8,128)(2,1)}, bf16[1024,384]{1,0:T(8,128)(2,1)}, u32[]{:S(2)}, u32[]{:S(2)}) %collective-permute-start.3) | collective-permute-done | bytes 786464 | tf_op jit(solution)/shard_map/ppermute | solution.py:18
  183.8 14.8 %collective-permute-done.4 = bf16[1024,384]{1,0:T(8,128)(2,1)} collective-permute-done((bf16[1024,384]{1,0:T(8,128)(2,1)}, bf16[1024,384]{1,0:T(8,128)(2,1)}, u32[]{:S(2)}, u32[]{:S(2)}) %collective-permute-start.4) | collective-permute-done | bytes 786464 | tf_op jit(solution)/shard_map/ppermute | solution.py:18
  201.3 48.4 %collective-permute-done.5 = bf16[1024,384]{1,0:T(8,128)(2,1)} collective-permute-done((bf16[1024,384]{1,0:T(8,128)(2,1)}, bf16[1024,384]{1,0:T(8,128)(2,1)}, u32[]{:S(2)}, u32[]{:S(2)}) %collective-permute-start.5) | collective-permute-done | bytes 786464 | tf_op jit(solution)/shard_map/ppermute | solution.py:18
  266.3 15.3 %fusion.106 = f32[1536,768]{0,1:T(8,128)S(1)} fusion(bf16[1536,4096]{1,0:T(8,128)(2,1)} %all-gather.5.cloned.1.call-done, bf16[4096,768]{1,0:T(8,128)(2,1)} %copy-done), kind=kOutput, calls=%fused_computation.209 | convolution fusion | flops 9663676416 | bytes 23592960 | tf_op jit(solution)/shard_map/dot_general | solution.py:10
  285.5 17.5 %all-gather.7.cloned.1.call-done = bf16[1536,4096]{1,0:T(8,128)(2,1)} async-done(((bf16[192,4096]{1,0:T(8,128)(2,1)}), bf16[1536,4096]{1,0:T(8,128)(2,1)}) %all-gather.7.cloned.1.call-update) | async-done | bytes 12582928 | tf_op jit(solution)/shard_map/all_gather | solution.py:123
  303.0 5.2 multiply_convert_fusion.8
  331.4 7.4 %convolution_convert_fusion.2 = bf16[2048,2048]{1,0:T(8,128)(2,1)} fusion(bf16[384,512]{1,0:T(8,128)(2,1)S(1)} %get-tuple-element.116, bf16[384,512]{1,0:T(8,128)(2,1)S(1)} %get-tuple-element.117, bf16[384,512]{1,0:T(8,128)(2,1)S(1)} %get-tuple-element.118, bf16[384,512]{1,0:T(8,128)(2,1)S(1)} %get-tuple-element.119, bf16[512,384]{0,1:T(8,128)(2,1)S(1)} %copy-done.40, ...), kind=kOutput, calls=%fused_computation.2 | convolution fusion | flops 3238002688 | bytes 11534336 | tf_op jit(solution)/shard_map/dot_general | solution.py:10
  343.2 8.6 %multiply_convert_fusion.4 = (bf16[1536,384]{0,1:T(8,128)(2,1)S(1)}, bf16[1536,384]{0,1:T(8,128)(2,1)S(1)}) fusion(f32[1536,768]{0,1:T(8,128)S(1)} %bitcast.61, bf16[1536,4096]{1,0:T(8,128)(2,1)} %all-gather.7.cloned.1.call-done, bf16[384,4096]{1,0:T(8,128)(2,1)S(1)} %constant_dynamic-update-slice_fusion), kind=kOutput, calls=%fused_computation.45 | convolution fusion | flops 4839505920 | bytes 22806528 | tf_op jit(solution)/shard_map/dot_general | solution.py:10
  351.9 7.2 convolution_convert_fusion.3
  364.9 5.9 add_convert_fusion.2
  389.3 8.8 %pad_maximum_fusion = bf16[2048,768]{0,1:T(8,128)(2,1)S(1)} fusion(bf16[512,768]{0,1:T(8,128)(2,1)S(1)} %copy-done.11, bf16[512,384]{0,1:T(8,128)(2,1)S(1)} %get-tuple-element.137, bf16[512,384]{0,1:T(8,128)(2,1)S(1)} %get-tuple-element.136, bf16[512,768]{0,1:T(8,128)(2,1)S(1)} %copy-done.12, bf16[512,768]{0,1:T(8,128)(2,1)S(1)} %copy-done.13), kind=kLoop, calls=%fused_computation.8 | loop fusion | flops 15728640 | bytes 6291456 | tf_op jit(solution)/shard_map/concatenate | solution.py:175
  400.6 5.9 multiply_convert_fusion.2
  406.5 29.0 %collective-permute-done.22 = bf16[384,1024]{1,0:T(8,128)(2,1)} collective-permute-done((bf16[384,1024]{1,0:T(8,128)(2,1)}, bf16[384,1024]{1,0:T(8,128)(2,1)}, u32[]{:S(2)}, u32[]{:S(2)}) %collective-permute-start.22) | collective-permute-done | bytes 786464 | tf_op jit(solution)/shard_map/ppermute | solution.py:18
  435.5 11.4 %convolution_convert_fusion.1 = bf16[2048,2048]{1,0:T(8,128)(2,1)} fusion(bf16[2048,768]{0,1:T(8,128)(2,1)S(1)} %pad_maximum_fusion, bf16[512,768]{1,0:T(8,128)(2,1)S(1)} %copy-done.34, bf16[512,768]{1,0:T(8,128)(2,1)S(1)} %copy-done.35, bf16[512,768]{1,0:T(8,128)(2,1)S(1)} %copy-done.36, bf16[512,768]{1,0:T(8,128)(2,1)S(1)} %copy-done.37), kind=kOutput, calls=%fused_computation.1 | convolution fusion | flops 6459228160 | bytes 14680064 | tf_op jit(solution)/shard_map/dot_general | solution.py:10
  453.3 5.8 multiply_convert_fusion.1
  459.0 5.9 multiply_convert_fusion
  465.0 9.4 %convolution_convert_fusion = bf16[2048,2048]{1,0:T(8,128)(2,1)S(1)} fusion(bf16[2048,768]{0,1:T(8,128)(2,1)S(1)} %pad_maximum_fusion, bf16[512,768]{1,0:T(8,128)(2,1)S(1)} %copy-done.31, bf16[512,768]{1,0:T(8,128)(2,1)S(1)} %copy-done.32, bf16[512,768]{1,0:T(8,128)(2,1)S(1)} %copy-done.33, bf16[512,768]{1,0:T(8,128)(2,1)S(1)} %copy-done.30), kind=kOutput, calls=%fused_computation | convolution fusion | flops 6459228160 | bytes 14680064 | tf_op jit(solution)/shard_map/dot_general | solution.py:10
  500.1 26.7 %collective-permute-done.24 = bf16[1024,1024]{1,0:T(8,128)(2,1)S(1)} collective-permute-done((bf16[1024,1024]{1,0:T(8,128)(2,1)S(1)}, bf16[1024,1024]{1,0:T(8,128)(2,1)S(1)}, u32[]{:S(2)}, u32[]{:S(2)}) %collective-permute-start.24) | collective-permute-done | bytes 2097184 | tf_op jit(solution)/shard_map/ppermute | solution.py:38
  539.9 18.6 %collective-permute-done.12 = bf16[1024,512]{1,0:T(8,128)(2,1)} collective-permute-done((bf16[1024,512]{1,0:T(8,128)(2,1)S(1)}, bf16[1024,512]{1,0:T(8,128)(2,1)}, u32[]{:S(2)}, u32[]{:S(2)}) %collective-permute-start.12) | collective-permute-done | bytes 1048608 | tf_op jit(solution)/shard_map/ppermute | solution.py:38
  558.5 4.7 add_convert_fusion.19
  565.1 15.0 %collective-permute-done.25 = bf16[1024,512]{1,0:T(8,128)(2,1)} collective-permute-done((bf16[1024,512]{1,0:T(8,128)(2,1)}, bf16[1024,512]{1,0:T(8,128)(2,1)}, u32[]{:S(2)}, u32[]{:S(2)}) %collective-permute-start.25) | collective-permute-done | bytes 1048608 | tf_op jit(solution)/shard_map/ppermute | solution.py:38
  584.1 6.3 add_multiply_fusion
  592.0 45.3 %collective-permute-done.30 = bf16[1024,768]{1,0:T(8,128)(2,1)} collective-permute-done((bf16[1024,768]{1,0:T(8,128)(2,1)}, bf16[1024,768]{1,0:T(8,128)(2,1)}, u32[]{:S(2)}, u32[]{:S(2)}) %collective-permute-start.30) | collective-permute-done | bytes 1572896 | tf_op jit(solution)/shard_map/ppermute | solution.py:18
  649.9 7.7 %collective-permute-done.15 = bf16[512,512]{1,0:T(8,128)(2,1)S(1)} collective-permute-done((bf16[512,512]{1,0:T(8,128)(2,1)S(1)}, bf16[512,512]{1,0:T(8,128)(2,1)S(1)}, u32[]{:S(2)}, u32[]{:S(2)}) %collective-permute-start.15) | collective-permute-done | bytes 524320 | tf_op jit(solution)/shard_map/ppermute | solution.py:22
  658.5 5.0 collective-permute-start.17
  663.5 5.2 collective-permute-done.31
  669.7 5.0 collective-permute-start.33
  675.2 4.8 collective-permute-done.17
  681.6 5.0 collective-permute-start.19
  692.8 5.0 collective-permute-start.35
  706.3 6.5 collective-permute-done.35
  (253 shorter events, 192.9 us)
Async XLA Ops:
  7.2 145.3 %all-gather.9.cloned.1.call-start = ((), (), s32[]{:S(2)}) async-start(), calls=%async_computation.2 | async-start | bytes 5242880 | tf_op jit(solution)/shard_map/all_gather | solution.py:116
  9.7 256.5 %all-gather.5.cloned.1.call-start = ((), (), s32[]{:S(2)}) async-start(), calls=%async_computation | async-start | bytes 14155776 | tf_op jit(solution)/shard_map/all_gather | solution.py:123
  11.3 145.4 %collective-permute-start = (bf16[1024,384]{1,0:T(8,128)(2,1)}, bf16[1024,384]{1,0:T(8,128)(2,1)}, u32[]{:S(2)}, u32[]{:S(2)}) collective-permute-start(bf16[1024,384]{1,0:T(8,128)(2,1)} %get-tuple-element.132), channel_id=1, source_target_pairs={{0,1},{1,2},{2,3},{3,0},{4,5},{5,6},{6,7},{7,4},{8,9},{9,10},{10,1... | collective-permute-start | bytes 2359304 | tf_op jit(solution)/shard_map/ppermute | solution.py:18
  14.4 142.4 %collective-permute-start.1 = (bf16[1024,384]{1,0:T(8,128)(2,1)}, bf16[1024,384]{1,0:T(8,128)(2,1)}, u32[]{:S(2)}, u32[]{:S(2)}) collective-permute-start(bf16[1024,384]{1,0:T(8,128)(2,1)} %get-tuple-element.131), channel_id=1, source_target_pairs={{0,3},{1,0},{2,1},{3,2},{4,7},{5,4},{6,5},{7,6},{8,11},{9,8},{10,9... | collective-permute-start | bytes 2359304 | tf_op jit(solution)/shard_map/ppermute | solution.py:18
  16.4 140.4 %collective-permute-start.2 = (bf16[1024,384]{1,0:T(8,128)(2,1)}, bf16[1024,384]{1,0:T(8,128)(2,1)}, u32[]{:S(2)}, u32[]{:S(2)}) collective-permute-start(bf16[1024,384]{1,0:T(8,128)(2,1)} %get-tuple-element.130), channel_id=1, source_target_pairs={{0,2},{1,3},{2,0},{3,1},{4,6},{5,7},{6,4},{7,5},{8,10},{9,11},{10,... | collective-permute-start | bytes 2359304 | tf_op jit(solution)/shard_map/ppermute | solution.py:18
  156.8 146.2 %all-gather.7.cloned.1.call-start = ((), (), s32[]{:S(2)}) async-start(), calls=%async_computation.1 | async-start | bytes 14155776 | tf_op jit(solution)/shard_map/all_gather | solution.py:123
  161.2 22.6 %collective-permute-start.3 = (bf16[1024,384]{1,0:T(8,128)(2,1)}, bf16[1024,384]{1,0:T(8,128)(2,1)}, u32[]{:S(2)}, u32[]{:S(2)}) collective-permute-start(bf16[1024,384]{1,0:T(8,128)(2,1)} %get-tuple-element.45), channel_id=1, source_target_pairs={{0,1},{1,2},{2,3},{3,0},{4,5},{5,6},{6,7},{7,4},{8,9},{9,10},{10,1... | collective-permute-start | bytes 2359304 | tf_op jit(solution)/shard_map/ppermute | solution.py:18
  161.2 37.3 %collective-permute-start.4 = (bf16[1024,384]{1,0:T(8,128)(2,1)}, bf16[1024,384]{1,0:T(8,128)(2,1)}, u32[]{:S(2)}, u32[]{:S(2)}) collective-permute-start(bf16[1024,384]{1,0:T(8,128)(2,1)} %get-tuple-element.46), channel_id=1, source_target_pairs={{0,3},{1,0},{2,1},{3,2},{4,7},{5,4},{6,5},{7,6},{8,11},{9,8},{10,9... | collective-permute-start | bytes 2359304 | tf_op jit(solution)/shard_map/ppermute | solution.py:18
  165.1 84.7 %collective-permute-start.5 = (bf16[1024,384]{1,0:T(8,128)(2,1)}, bf16[1024,384]{1,0:T(8,128)(2,1)}, u32[]{:S(2)}, u32[]{:S(2)}) collective-permute-start(bf16[1024,384]{1,0:T(8,128)(2,1)} %get-tuple-element.47), channel_id=1, source_target_pairs={{0,2},{1,3},{2,0},{3,1},{4,6},{5,7},{6,4},{7,5},{8,10},{9,11},{10,... | collective-permute-start | bytes 2359304 | tf_op jit(solution)/shard_map/ppermute | solution.py:18
  183.8 133.0 %collective-permute-start.6 = (bf16[384,1024]{1,0:T(8,128)(2,1)}, bf16[384,1024]{1,0:T(8,128)(2,1)}, u32[]{:S(2)}, u32[]{:S(2)}) collective-permute-start(bf16[384,1024]{1,0:T(8,128)(2,1)} %get-tuple-element.52), channel_id=1, source_target_pairs={{0,1},{1,2},{2,3},{3,0},{4,5},{5,6},{6,7},{7,4},{8,9},{9,10},{10,1... | collective-permute-start | bytes 2359304 | tf_op jit(solution)/shard_map/ppermute | solution.py:18
  198.6 118.2 %collective-permute-start.7 = (bf16[384,1024]{1,0:T(8,128)(2,1)}, bf16[384,1024]{1,0:T(8,128)(2,1)}, u32[]{:S(2)}, u32[]{:S(2)}) collective-permute-start(bf16[384,1024]{1,0:T(8,128)(2,1)} %get-tuple-element.54), channel_id=1, source_target_pairs={{0,3},{1,0},{2,1},{3,2},{4,7},{5,4},{6,5},{7,6},{8,11},{9,8},{10,9... | collective-permute-start | bytes 2359304 | tf_op jit(solution)/shard_map/ppermute | solution.py:18
  249.7 67.0 %collective-permute-start.8 = (bf16[384,1024]{1,0:T(8,128)(2,1)}, bf16[384,1024]{1,0:T(8,128)(2,1)}, u32[]{:S(2)}, u32[]{:S(2)}) collective-permute-start(bf16[384,1024]{1,0:T(8,128)(2,1)} %get-tuple-element.56), channel_id=1, source_target_pairs={{0,2},{1,3},{2,0},{3,1},{4,6},{5,7},{6,4},{7,5},{8,10},{9,11},{10,... | collective-permute-start | bytes 2359304 | tf_op jit(solution)/shard_map/ppermute | solution.py:18
  338.8 26.1 %collective-permute-start.9 = (bf16[2048,2048]{1,0:T(8,128)(2,1)}, bf16[2048,2048]{1,0:T(8,128)(2,1)}, u32[]{:S(2)}, u32[]{:S(2)}) collective-permute-start(bf16[2048,2048]{1,0:T(8,128)(2,1)} %convolution_convert_fusion.2), channel_id=1, source_target_pairs={{0,4},{4,0},{8,12},{12,8},{16,20},{20,16},{24,28},{28,24},{1,5},{5... | collective-permute-start | bytes 25165832 | tf_op jit(solution)/shard_map/ppermute | solution.py:38
  341.7 29.1 %collective-permute-start.10 = (bf16[384,1024]{1,0:T(8,128)(2,1)}, bf16[384,1024]{1,0:T(8,128)(2,1)}, u32[]{:S(2)}, u32[]{:S(2)}) collective-permute-start(bf16[384,1024]{1,0:T(8,128)(2,1)} %multiply_convert_fusion.8), channel_id=1, source_target_pairs={{0,1},{1,2},{2,3},{3,0},{4,5},{5,6},{6,7},{7,4},{8,9},{9,10},{10,1... | collective-permute-start | bytes 2359304 | tf_op jit(solution)/shard_map/ppermute | solution.py:18
  370.7 64.7 %collective-permute-start.11 = (bf16[1024,1024]{1,0:T(8,128)(2,1)}, bf16[1024,1024]{1,0:T(8,128)(2,1)}, u32[]{:S(2)}, u32[]{:S(2)}) collective-permute-start(bf16[1024,1024]{1,0:T(8,128)(2,1)} %get-tuple-element.59), channel_id=1, source_target_pairs={{0,16},{4,20},{8,24},{12,28},{16,0},{20,4},{24,8},{28,12},{1,17},{... | collective-permute-start | bytes 6291464 | tf_op jit(solution)/shard_map/ppermute | solution.py:38
  371.7 63.7 %collective-permute-start.13 = (bf16[1024,1024]{1,0:T(8,128)(2,1)}, bf16[1024,1024]{1,0:T(8,128)(2,1)}, u32[]{:S(2)}, u32[]{:S(2)}) collective-permute-start(bf16[1024,1024]{1,0:T(8,128)(2,1)} %get-tuple-element.60), channel_id=1, source_target_pairs={{0,8},{4,12},{8,0},{12,4},{16,24},{20,28},{24,16},{28,20},{1,9},{5... | collective-permute-start | bytes 6291464 | tf_op jit(solution)/shard_map/ppermute | solution.py:38
  381.2 25.2 %collective-permute-start.21 = (bf16[384,1024]{1,0:T(8,128)(2,1)}, bf16[384,1024]{1,0:T(8,128)(2,1)}, u32[]{:S(2)}, u32[]{:S(2)}) collective-permute-start(bf16[384,1024]{1,0:T(8,128)(2,1)} %multiply_convert_fusion.7), channel_id=1, source_target_pairs={{0,3},{1,0},{2,1},{3,2},{4,7},{5,4},{6,5},{7,6},{8,11},{9,8},{10,9... | collective-permute-start | bytes 2359304 | tf_op jit(solution)/shard_map/ppermute | solution.py:18
  384.0 51.5 %collective-permute-start.22 = (bf16[384,1024]{1,0:T(8,128)(2,1)}, bf16[384,1024]{1,0:T(8,128)(2,1)}, u32[]{:S(2)}, u32[]{:S(2)}) collective-permute-start(bf16[384,1024]{1,0:T(8,128)(2,1)} %multiply_convert_fusion.6), channel_id=1, source_target_pairs={{0,2},{1,3},{2,0},{3,1},{4,6},{5,7},{6,4},{7,5},{8,10},{9,11},{10,... | collective-permute-start | bytes 2359304 | tf_op jit(solution)/shard_map/ppermute | solution.py:18
  446.9 27.6 %collective-permute-start.23 = (bf16[2048,2048]{1,0:T(8,128)(2,1)}, bf16[2048,2048]{1,0:T(8,128)(2,1)}, u32[]{:S(2)}, u32[]{:S(2)}) collective-permute-start(bf16[2048,2048]{1,0:T(8,128)(2,1)} %convolution_convert_fusion.1), channel_id=1, source_target_pairs={{0,4},{4,0},{8,12},{12,8},{16,20},{20,16},{24,28},{28,24},{1,5},{5... | collective-permute-start | bytes 25165832 | tf_op jit(solution)/shard_map/ppermute | solution.py:38
  448.1 46.1 %collective-permute-start.28 = (bf16[1024,768]{1,0:T(8,128)(2,1)}, bf16[1024,768]{1,0:T(8,128)(2,1)}, u32[]{:S(2)}, u32[]{:S(2)}) collective-permute-start(bf16[1024,768]{1,0:T(8,128)(2,1)} %multiply_convert_fusion.2), channel_id=1, source_target_pairs={{0,1},{1,2},{2,3},{3,0},{4,5},{5,6},{6,7},{7,4},{8,9},{9,10},{10,1... | collective-permute-start | bytes 4718600 | tf_op jit(solution)/shard_map/ppermute | solution.py:18
  478.9 47.9 %collective-permute-start.24 = (bf16[1024,1024]{1,0:T(8,128)(2,1)S(1)}, bf16[1024,1024]{1,0:T(8,128)(2,1)S(1)}, u32[]{:S(2)}, u32[]{:S(2)}) collective-permute-start(bf16[1024,1024]{1,0:T(8,128)(2,1)S(1)} %get-tuple-element.74), channel_id=1, source_target_pairs={{0,16},{4,20},{8,24},{12,28},{16,0},{20,4},{24,8},{28,12},{1,17},{... | collective-permute-start | bytes 6291464 | tf_op jit(solution)/shard_map/ppermute | solution.py:38
  487.2 76.6 %collective-permute-start.26 = (bf16[1024,1024]{1,0:T(8,128)(2,1)}, bf16[1024,1024]{1,0:T(8,128)(2,1)S(1)}, u32[]{:S(2)}, u32[]{:S(2)}) collective-permute-start(bf16[1024,1024]{1,0:T(8,128)(2,1)} %get-tuple-element.75), channel_id=1, source_target_pairs={{0,8},{4,12},{8,0},{12,4},{16,24},{20,28},{24,16},{28,20},{1,9},{5... | collective-permute-start | bytes 6291464 | tf_op jit(solution)/shard_map/ppermute | solution.py:38
  497.9 60.6 %collective-permute-start.12 = (bf16[1024,512]{1,0:T(8,128)(2,1)S(1)}, bf16[1024,512]{1,0:T(8,128)(2,1)}, u32[]{:S(2)}, u32[]{:S(2)}) collective-permute-start(bf16[1024,512]{1,0:T(8,128)(2,1)S(1)} %add_convert_fusion.20), channel_id=1, source_target_pairs={{0,8},{4,12},{8,0},{12,4},{16,24},{20,28},{24,16},{28,20},{1,9},{5... | collective-permute-start | bytes 3145736 | tf_op jit(solution)/shard_map/ppermute | solution.py:38
  530.2 49.9 %collective-permute-start.25 = (bf16[1024,512]{1,0:T(8,128)(2,1)}, bf16[1024,512]{1,0:T(8,128)(2,1)}, u32[]{:S(2)}, u32[]{:S(2)}) collective-permute-start(bf16[1024,512]{1,0:T(8,128)(2,1)} %add_convert_fusion.10), channel_id=1, source_target_pairs={{0,8},{4,12},{8,0},{12,4},{16,24},{20,28},{24,16},{28,20},{1,9},{5... | collective-permute-start | bytes 3145736 | tf_op jit(solution)/shard_map/ppermute | solution.py:38
  532.1 58.2 %collective-permute-start.29 = (bf16[1024,768]{1,0:T(8,128)(2,1)}, bf16[1024,768]{1,0:T(8,128)(2,1)}, u32[]{:S(2)}, u32[]{:S(2)}) collective-permute-start(bf16[1024,768]{1,0:T(8,128)(2,1)} %multiply_convert_fusion.1), channel_id=1, source_target_pairs={{0,3},{1,0},{2,1},{3,2},{4,7},{5,4},{6,5},{7,6},{8,11},{9,8},{10,9... | collective-permute-start | bytes 4718600 | tf_op jit(solution)/shard_map/ppermute | solution.py:18
  535.9 101.4 %collective-permute-start.30 = (bf16[1024,768]{1,0:T(8,128)(2,1)}, bf16[1024,768]{1,0:T(8,128)(2,1)}, u32[]{:S(2)}, u32[]{:S(2)}) collective-permute-start(bf16[1024,768]{1,0:T(8,128)(2,1)} %multiply_convert_fusion), channel_id=1, source_target_pairs={{0,2},{1,3},{2,0},{3,1},{4,6},{5,7},{6,4},{7,5},{8,10},{9,11},{10,... | collective-permute-start | bytes 4718600 | tf_op jit(solution)/shard_map/ppermute | solution.py:18
  563.2 75.9 %collective-permute-start.14 = (bf16[1024,512]{1,0:T(8,128)(2,1)}, bf16[1024,512]{1,0:T(8,128)(2,1)}, u32[]{:S(2)}, u32[]{:S(2)}) collective-permute-start(bf16[1024,512]{1,0:T(8,128)(2,1)} %get-tuple-element.90), channel_id=1, source_target_pairs={{0,16},{4,20},{8,24},{12,28},{16,0},{20,4},{24,8},{28,12},{1,17},{... | collective-permute-start | bytes 3145736 | tf_op jit(solution)/shard_map/ppermute | solution.py:38
  583.4 61.8 %collective-permute-start.27 = (bf16[1024,512]{1,0:T(8,128)(2,1)S(1)}, bf16[1024,512]{1,0:T(8,128)(2,1)S(1)}, u32[]{:S(2)}, u32[]{:S(2)}) collective-permute-start(bf16[1024,512]{1,0:T(8,128)(2,1)S(1)} %get-tuple-element.86), channel_id=1, source_target_pairs={{0,16},{4,20},{8,24},{12,28},{16,0},{20,4},{24,8},{28,12},{1,17},{... | collective-permute-start | bytes 3145736 | tf_op jit(solution)/shard_map/ppermute | solution.py:38
  648.1 20.6 %collective-permute-start.31 = (bf16[512,512]{1,0:T(8,128)(2,1)S(1)}, bf16[512,512]{1,0:T(8,128)(2,1)S(1)}, u32[]{:S(2)}, u32[]{:S(2)}) collective-permute-start(bf16[512,512]{1,0:T(8,128)(2,1)S(1)} %get-tuple-element.79), channel_id=1, source_target_pairs={{0,1},{4,5},{8,9},{12,13},{16,17},{20,21},{24,25},{28,29}} | collective-permute-start | bytes 1572872 | tf_op jit(solution)/shard_map/ppermute | solution.py:22
  658.5 21.5 %collective-permute-start.17 = (bf16[512,512]{1,0:T(8,128)(2,1)S(1)}, bf16[512,512]{1,0:T(8,128)(2,1)S(1)}, u32[]{:S(2)}, u32[]{:S(2)}) collective-permute-start(bf16[512,512]{1,0:T(8,128)(2,1)S(1)} %get-tuple-element.63), channel_id=1, source_target_pairs={{0,1},{1,2},{4,5},{5,6},{8,9},{9,10},{12,13},{13,14},{16,17},{17,1... | collective-permute-start | bytes 1572872 | tf_op jit(solution)/shard_map/ppermute | solution.py:22
  669.7 21.5 %collective-permute-start.33 = (bf16[512,512]{1,0:T(8,128)(2,1)S(1)}, bf16[512,512]{1,0:T(8,128)(2,1)S(1)}, u32[]{:S(2)}, u32[]{:S(2)}) collective-permute-start(bf16[512,512]{1,0:T(8,128)(2,1)S(1)} %get-tuple-element.81), channel_id=1, source_target_pairs={{0,1},{1,2},{4,5},{5,6},{8,9},{9,10},{12,13},{13,14},{16,17},{17,1... | collective-permute-start | bytes 1572872 | tf_op jit(solution)/shard_map/ppermute | solution.py:22
  681.6 20.9 %collective-permute-start.19 = (bf16[512,512]{1,0:T(8,128)(2,1)S(1)}, bf16[512,512]{1,0:T(8,128)(2,1)S(1)}, u32[]{:S(2)}, u32[]{:S(2)}) collective-permute-start(bf16[512,512]{1,0:T(8,128)(2,1)S(1)} %get-tuple-element.65), channel_id=1, source_target_pairs={{0,1},{1,2},{2,3},{4,5},{5,6},{6,7},{8,9},{9,10},{10,11},{12,13},{... | collective-permute-start | bytes 1572872 | tf_op jit(solution)/shard_map/ppermute | solution.py:22
  (61 other events, 652.5 us)
Sparse Core Ops, SparseCore 0:
  10.2 142.2 all-gather.8
  157.0 71.3 all-gather.4
  230.9 72.1 all-gather.6
